TPU v7x, 32 devices: a whole 2x2x4 slice. The times are simulated.
32 devices in a mesh: box: 8 (over y, x, core), dir: 4 (over z).
Axes of the slice: x: 2, y: 2, z: 4, core: 2. Of those that a mesh axis runs over, the one named last changes fastest.
Arguments:
- fine_out: float32 [1024, 2, 8192], P(('box', 'dir')), may hold values from -6 to 6
- theta_interp: float32 [128, 64], replicated, may hold values from -0.75 to 0.75
- phi_interp: float32 [128, 256], replicated, may hold values from -0.5 to 0.5
- shift_phase: float32 [8, 32768], P(None, 'dir'), may hold values from -3.140625 to 3.140625
- translation: float32 [316, 2, 32768], P(None, None, 'dir'), may hold values from -0.25 to 0.25
- upper_in: float32 [128, 2, 32768], P('box', None, 'dir'), may hold values from -6 to 6
- children: int32 [128, 8], P('box'), may hold values from 0 to 1023, as said below
- far_boxes: int32 [128, 28], P('box'), may hold values from 0 to 127, as said below
- far_offsets: int32 [128, 28], P('box'), may hold values from 0 to 315
Outputs:
- coarse_in: float32 [128, 2, 32768], P('box', None, 'dir')
- fine_in: float32 [1024, 2, 8192], P(('box', 'dir'))
Inputs may be any that keep to these rules, and one draw needn't show every extreme that they name: Every fine box is named exactly once. The coarse boxes i * 16 to (i + 1) * 16 - 1 have as children exactly the fine boxes 8 * i * 16 to 8 * (i + 1) * 16 - 1. `far_boxes`: each row names 28 different coarse boxes, never the row's own box.
All inputs are finite; a program needn't handle non-finite values.
Results may differ from a plain program's by a relative error of at most 0.00008.
Values sent between devices are 32-bit elements; how exact they have to be, the bound alone decides.
A program may use at most 192 MiB of HBM per device.

v0:
```python
import functools

import jax
import jax.numpy as jnp
from jax import lax
from jax.experimental import pallas as pl
from jax.experimental.pallas import tpu as pltpu
from jax.sharding import PartitionSpec as P

F32, BF16 = jnp.float32, jnp.bfloat16
VMEM_BYTES = 52 * 1024 * 1024
CHUNKS = 2


def split(x):
    hi = x.astype(BF16)
    return hi, (x - hi.astype(F32)).astype(BF16)


def dot3(a, b):
    (ah, al), (bh, bl) = a, b
    d = functools.partial(jnp.dot, preferred_element_type=F32)
    return d(ah, bh) + (d(ah, bl) + d(al, bh))


def rows_view(x):
    n, _, k = x.shape
    return x.reshape(n, 2, k // 128, 128).transpose(0, 2, 1, 3).reshape(n, k // 64, 128)


def rows_unview(x):
    n, r, _ = x.shape
    return x.reshape(n, r // 2, 2, 128).transpose(0, 2, 1, 3).reshape(n, 2, r * 64)


def gather_up_kernel(group, parent, octant, x_ref, theta_ref, phi_ref, cs_ref, *out_refs):
    step = pl.program_id(0)
    nd, tl = cs_ref.shape[0], cs_ref.shape[3]
    tlc = tl // len(out_refs)
    tc = nd * tl

    @pl.when(step == 0)
    def _():
        for out_ref in out_refs:
            out_ref[...] = jnp.zeros_like(out_ref)

    theta = split(theta_ref[...])
    phi = split(phi_ref[...])
    rows = x_ref.shape[1]
    along = dot3(split(x_ref[...].reshape(group * rows, x_ref.shape[2])), phi)
    for g in range(group):
        p, o = parent[step * group + g], octant[step * group + g]
        full = dot3(theta, split(along[g * rows : (g + 1) * rows]))
        for j in range(nd):
            for h, out_ref in enumerate(out_refs):
                first = j * tl + h * tlc
                re = full[first : first + tlc]
                im = full[tc + first : tc + first + tlc]
                c = cs_ref[j, 0, o, h * tlc : (h + 1) * tlc]
                s = cs_ref[j, 1, o, h * tlc : (h + 1) * tlc]
                out_ref[j, p, 0] += c * re - s * im
                out_ref[j, p, 1] += s * re + c * im


def gather_up(x, theta2, phi, cs, parent, octant, parents):
    n, rows, lanes = x.shape
    nd, _, _, tl, pc = cs.shape
    shape = (nd, parents, 2, tl // CHUNKS, pc)
    group = 4
    return pl.pallas_call(
        functools.partial(gather_up_kernel, group),
        grid_spec=pltpu.PrefetchScalarGridSpec(
            num_scalar_prefetch=2,
            grid=(n // group,),
            in_specs=[
                pl.BlockSpec((group, rows, lanes), lambda i, *_: (i, 0, 0)),
                pl.BlockSpec(theta2.shape, lambda i, *_: (0, 0)),
                pl.BlockSpec(phi.shape, lambda i, *_: (0, 0)),
                pl.BlockSpec(cs.shape, lambda i, *_: (0, 0, 0, 0, 0)),
            ],
            out_specs=[pl.BlockSpec(shape, lambda i, *_: (0, 0, 0, 0, 0))] * CHUNKS,
        ),
        out_shape=[jax.ShapeDtypeStruct(shape, F32)] * CHUNKS,
        compiler_params=pltpu.CompilerParams(vmem_limit_bytes=VMEM_BYTES),
    )(parent, octant, x, theta2, phi, cs)


def translate_kernel(chunk, far, kind, q_ref, trans_ref, upper_ref, *refs):
    rows_ref, plane_ref, buf, sem = refs[-4:]
    p = pl.program_id(0)
    count, many = pl.num_programs(0), far.shape[1]
    tl = q_ref.shape[2]
    part = pl.ds(chunk * buf.shape[2], buf.shape[2])

    def start(row, slot):
        for l in range(many):
            pltpu.make_async_copy(
                trans_ref.at[kind[row, l], part], buf.at[slot, l], sem.at[slot]
            ).start()

    @pl.when(p == 0)
    def _():
        start(0, 0)

    @pl.when(p + 1 < count)
    def _():
        start(p + 1, (p + 1) % 2)

    slot = p % 2
    pltpu.make_async_copy(trans_ref.at[pl.ds(0, many), part], buf.at[slot], sem.at[slot]).wait()
    for t in range(0, tl, 8):
        for h in range(2):
            re = im = None
            for l in range(many):
                f = far[p, l]
                q0 = q_ref[f, 0, t : t + 8, h * 128 : (h + 1) * 128]
                q1 = q_ref[f, 1, t : t + 8, h * 128 : (h + 1) * 128]
                a0 = buf[slot, l, pl.ds(t * 4 + h * 2, 8, stride=4), :]
                a1 = buf[slot, l, pl.ds(t * 4 + h * 2 + 1, 8, stride=4), :]
                r, i = a0 * q0 - a1 * q1, a0 * q1 + a1 * q0
                re = r if re is None else re + r
                im = i if im is None else im + i
            for c, total in ((0, re), (1, im)):
                where = pl.ds(t * 4 + h * 2 + c, 8, stride=4)
                total = total + upper_ref[0, where, :]
                rows_ref[0, where, :] = total
                plane_ref[0, c, t : t + 8, h * 128 : (h + 1) * 128] = total


def translate(chunk, q, trans, upper, far, kind, before):
    parents, all_rows, lanes = upper.shape
    rows = all_rows // CHUNKS
    _, _, tl, pc = q.shape
    many = far.shape[1]
    return pl.pallas_call(
        functools.partial(translate_kernel, chunk),
        grid_spec=pltpu.PrefetchScalarGridSpec(
            num_scalar_prefetch=2,
            grid=(parents,),
            in_specs=[
                pl.BlockSpec(q.shape, lambda i, *_: (0, 0, 0, 0)),
                pl.BlockSpec(memory_space=pl.ANY),
                pl.BlockSpec((1, rows, lanes), lambda i, *_: (i, chunk, 0)),
            ]
            + [pl.BlockSpec(memory_space=pl.ANY)] * len(before),
            out_specs=[
                pl.BlockSpec((1, rows, lanes), lambda i, *_: (i, chunk, 0)),
                pl.BlockSpec((1, 2, tl, pc), lambda i, *_: (i, 0, 0, 0)),
            ],
            scratch_shapes=[
                pltpu.VMEM((2, many, rows, lanes), F32),
                pltpu.SemaphoreType.DMA((2,)),
            ],
        ),
        out_shape=[
            jax.ShapeDtypeStruct((parents, all_rows, lanes), F32),
            jax.ShapeDtypeStruct((parents, 2, tl, pc), F32),
        ],
        compiler_params=pltpu.CompilerParams(vmem_limit_bytes=VMEM_BYTES),
        input_output_aliases={5: 0} if before else {},
    )(far, kind, q, trans, upper, *before)


def spread_down_kernel(group, parent, octant, *refs):
    in_refs, (theta_ref, phi_ref, cs_ref, out_ref, full) = refs[:-5], refs[-5:]
    step = pl.program_id(0)
    nd, tl = cs_ref.shape[0], cs_ref.shape[3]
    tlc = tl // len(in_refs)
    tc = nd * tl
    theta = split(theta_ref[...])
    phi = split(phi_ref[...])
    parts = []
    for g in range(group):
        p, o = parent[step * group + g], octant[step * group + g]
        for j in range(nd):
            for h, in_ref in enumerate(in_refs):
                first = j * tl + h * tlc
                re, im = in_ref[j, p, 0], in_ref[j, p, 1]
                c = cs_ref[j, 0, o, h * tlc : (h + 1) * tlc]
                s = cs_ref[j, 1, o, h * tlc : (h + 1) * tlc]
                full[g, first : first + tlc] = c * re + s * im
                full[g, tc + first : tc + first + tlc] = c * im - s * re
        parts.append(dot3(theta, split(full[g])))
    along = jnp.concatenate(parts, axis=0)
    out_ref[...] = dot3(split(along), phi).reshape(out_ref.shape)


def spread_down(incoming, theta2t, phit, cs, parent, octant):
    nd, _, _, tl, pc = cs.shape
    n = parent.shape[0]
    rows, lanes = theta2t.shape[0], phit.shape[1]
    group = 4
    return pl.pallas_call(
        functools.partial(spread_down_kernel, group),
        grid_spec=pltpu.PrefetchScalarGridSpec(
            num_scalar_prefetch=2,
            grid=(n // group,),
            in_specs=[
                *(pl.BlockSpec(x.shape, lambda i, *_: (0, 0, 0, 0, 0)) for x in incoming),
                pl.BlockSpec(theta2t.shape, lambda i, *_: (0, 0)),
                pl.BlockSpec(phit.shape, lambda i, *_: (0, 0)),
                pl.BlockSpec(cs.shape, lambda i, *_: (0, 0, 0, 0, 0)),
            ],
            out_specs=pl.BlockSpec((group, rows, lanes), lambda i, *_: (i, 0, 0)),
            scratch_shapes=[pltpu.VMEM((group, 2 * nd * tl, pc), F32)],
        ),
        out_shape=jax.ShapeDtypeStruct((n, rows, lanes), F32),
        compiler_params=pltpu.CompilerParams(vmem_limit_bytes=VMEM_BYTES),
    )(parent, octant, *incoming, theta2t, phit, cs)


def box_bits():
    return range(lax.axis_size("box").bit_length() - 2, -1, -1)


def gather_box(x):
    nb = lax.axis_size("box")
    for bit in box_bits():
        other = lax.ppermute(x, "box", [(i, i ^ (1 << bit)) for i in range(nb)])
        x = jnp.concatenate([x, other], axis=0)
    return x


def box_place(box):
    apart = box ^ lax.axis_index("box")
    place = jnp.zeros_like(box)
    for stage, bit in enumerate(box_bits()):
        place = place + (((apart >> bit) & 1) << stage)
    return place


def shards(
    fine_out,
    theta_interp,
    phi_interp,
    shift_phase,
    translation,
    upper_in,
    children,
    far_boxes,
    far_offsets,
):
    n = fine_out.shape[0]
    tc, tf = theta_interp.shape
    pc = phi_interp.shape[1]
    parents = children.shape[0]
    tl = shift_phase.shape[1] // pc
    nd = tc // tl
    flat = (children % (n * nd)).reshape(-1)
    own = lax.axis_index("dir") * n + jnp.arange(n, dtype=jnp.int32)
    slots = jnp.arange(flat.shape[0], dtype=jnp.int32)
    slot = jnp.sum(jnp.where(flat[None, :] == own[:, None], slots[None, :], 0), axis=1)
    parent, octant = slot // 8, slot % 8
    theta2 = (jnp.eye(2, dtype=F32)[:, None, None, :] * theta_interp[None, :, :, None]).reshape(
        2 * tc, 2 * tf
    )
    phases = lax.all_gather(shift_phase.reshape(8, tl, pc), "dir", axis=0)
    cs = jnp.stack([jnp.cos(phases), jnp.sin(phases)], axis=1)
    partials = gather_up(rows_view(fine_out), theta2, phi_interp, cs, parent, octant, parents)
    operators, upper = rows_view(translation), rows_view(upper_in)
    every_box = []
    for partial in partials:
        outgoing = lax.psum_scatter(
            partial.reshape((nd * parents * 2,) + partial.shape[3:]),
            "dir",
            scatter_dimension=0,
            tiled=True,
        ).reshape(partial.shape[1:])
        if every_box:
            every_box[-1], outgoing = lax.optimization_barrier((every_box[-1], outgoing))
        every_box.append(gather_box(outgoing))
    sources_at = box_place(far_boxes // parents) * parents + far_boxes % parents
    before, incoming = (), []
    for chunk, sources in enumerate(every_box):
        rows, planes = translate(
            chunk, sources, operators, upper, sources_at, far_offsets, before
        )
        before = (rows,)
        incoming.append(lax.all_gather(planes, "dir", axis=0))
    fine_in = spread_down(incoming, theta2.T, phi_interp.T, cs, parent, octant)
    return (rows_unview(rows), rows_unview(fine_in))


def solution(mesh):
    placed = (
        P(("box", "dir"), None, None),
        P(),
        P(),
        P(None, "dir"),
        P(None, None, "dir"),
        P("box", None, "dir"),
        P("box", None),
        P("box", None),
        P("box", None),
    )
    return jax.shard_map(
        shards,
        mesh=mesh,
        in_specs=placed,
        out_specs=(P("box", None, "dir"), P(("box", "dir"), None, None)),
        check_vma=False,
    )
```

profile of v0, /device:TPU:0, one launch (start us, length us, event | category | flops | bytes accessed | tf_op | source)
XLA Modules:
  0.0 292.9 jit_solution(2454090615385272910)
XLA Ops:
  7.2 0.0 all-gather.6.cloned.1.call-start
  7.2 1.7 copy.52
  8.9 0.0 all-gather.6.cloned.1.call-update
  9.0 0.0 reduce-scatter.3.cloned.1.call-start
  9.0 0.7 add_select_fusion.2
  9.7 0.1 copy.38
  9.8 0.1 eq.28
  9.9 0.9 broadcast_multiply_fusion
  10.8 0.1 copy.40.theta_ref
  10.9 0.2 select_reduce_fusion
  11.1 29.7 %all-gather.6.cloned.1.call-done = f32[4,8,32,256]{3,2,1,0:T(8,128)} async-done(((f32[1,8,32,256]{3,2,1,0:T(8,128)}), f32[4,8,32,256]{3,2,1,0:T(8,128)}) %all-gather.6.cloned.1.call-update) | async-done | bytes 1048592 | tf_op jit(solution)/shard_map/all_gather | solution.py:257
  40.8 4.7 %cosine_bitcast_fusion = (f32[4,1,8,32,256]{4,3,2,1,0:T(8,128)S(1)}, f32[4,1,8,32,256]{4,3,2,1,0:T(8,128)S(1)}) fusion(f32[4,8,32,256]{3,2,1,0:T(8,128)} %all-gather.6.cloned.1.call-done), kind=kLoop, calls=%fused_computation.8 | loop fusion | bytes 3145728 | tf_op jit(solution)/shard_map/stack | solution.py:258
  45.5 0.0 copy-start.1
  45.5 1.5 pad_maximum_fusion.2.cs_ref.refs_4_
  47.0 14.4 %shard_map.104 = (f32[4,16,2,16,256]{4,3,2,1,0:T(8,128)}, f32[4,16,2,16,256]{4,3,2,1,0:T(8,128)}) custom-call(s32[32]{0:T(128)S(1)} %get-tuple-element.23.parent, s32[32]{0:T(128)S(1)} %get-tuple-element.22.octant, f32[32,128,128]{2,1,0:T(8,128)} %bitcast.71, f32[256,128]{1,0:T(8,128)S(1)} %copy.40.theta_ref, f32[128,256]{1,0:T(8,128)S(1)} %copy-done.1, ...), custom_call_target="tpu_custom_call" | custom-call | tf_op jit(solution)/shard_map/pallas_call | solution.py:70
  61.4 0.0 reduce-scatter.3.cloned.1.call-update
  61.4 0.0 reduce-scatter.5.cloned.1.call-start
  61.5 0.7 reduce-scatter.5.cloned.1.call-update
  62.2 0.0 all-gather.8.cloned.1.call-start
  62.2 42.7 %reduce-scatter.3.cloned.1.call-done = f32[32,16,256]{2,1,0:T(8,128)} async-done(((f32[128,16,256]{2,1,0:T(8,128)}), f32[32,16,256]{2,1,0:T(8,128)}) %reduce-scatter.3.cloned.1.call-update) | async-done | bytes 524304 | tf_op jit(solution)/shard_map/reduce_scatter | solution.py:263
  104.9 1.5 collective-permute-start
  106.4 12.2 %collective-permute-done = f32[16,2,16,256]{3,2,1,0:T(8,128)S(1)} collective-permute-done((f32[16,2,16,256]{3,2,1,0:T(8,128)}, f32[16,2,16,256]{3,2,1,0:T(8,128)S(1)}, u32[]{:S(2)}, u32[]{:S(2)}) %collective-permute-start) | collective-permute-done | bytes 524320 | tf_op jit(solution)/shard_map/ppermute | solution.py:219
  118.6 1.2 pad_maximum_fusion.5
  119.8 1.5 collective-permute-start.1
  121.4 22.5 %collective-permute-done.1 = f32[32,2,16,256]{3,2,1,0:T(8,128)S(1)} collective-permute-done((f32[32,2,16,256]{3,2,1,0:T(8,128)S(1)}, f32[32,2,16,256]{3,2,1,0:T(8,128)S(1)}, u32[]{:S(2)}, u32[]{:S(2)}) %collective-permute-start.1) | collective-permute-done | bytes 1048608 | tf_op jit(solution)/shard_map/ppermute | solution.py:219
  143.8 0.2 pad_maximum_fusion.3
  144.0 0.1 collective-permute-start.2
  144.1 4.1 %collective-permute-done.2 = f32[64,2,16,256]{3,2,1,0:T(8,128)S(1)} collective-permute-done((f32[64,2,16,256]{3,2,1,0:T(8,128)S(1)}, f32[64,2,16,256]{3,2,1,0:T(8,128)S(1)}, u32[]{:S(2)}, u32[]{:S(2)}) %collective-permute-start.2) | collective-permute-done | bytes 2097184 | tf_op jit(solution)/shard_map/ppermute | solution.py:219
  148.3 2.4 pad_maximum_fusion.q_ref
  150.7 1.5 collective-permute-start.3
  152.2 12.7 %collective-permute-done.3 = f32[16,2,16,256]{3,2,1,0:T(8,128)S(1)} collective-permute-done((f32[16,2,16,256]{3,2,1,0:T(8,128)}, f32[16,2,16,256]{3,2,1,0:T(8,128)S(1)}, u32[]{:S(2)}, u32[]{:S(2)}) %collective-permute-start.3) | collective-permute-done | bytes 524320 | tf_op jit(solution)/shard_map/ppermute | solution.py:219
  164.9 2.2 pad_maximum_fusion.6
  167.1 1.5 collective-permute-start.4
  168.6 0.0 copy-done
  168.6 16.0 %shard_map.105 = (f32[16,128,128]{2,1,0:T(8,128)}, f32[16,2,16,256]{3,2,1,0:T(8,128)}) custom-call(s32[16,28]{1,0:T(8,128)S(1)} %fusion.1.far, s32[16,28]{1,0:T(8,128)S(1)} %copy-done.2, f32[128,2,16,256]{3,2,1,0:T(8,128)} %pad_maximum_fusion.q_ref, f32[316,128,128]{2,1,0:T(8,128)} %bitcast.58, f32[16,128,128]{2,1,0:T(8,128)S(1)} %bitcast.53), custom_call_target="tpu_custom_call" | custom-call | tf_op jit(solution)/shard_map/pallas_call | solution.py:135
  184.6 0.0 all-gather.8.cloned.1.call-update
  184.6 0.0 all-gather.10.cloned.1.call-start
  184.7 7.0 %collective-permute-done.4 = f32[32,2,16,256]{3,2,1,0:T(8,128)S(1)} collective-permute-done((f32[32,2,16,256]{3,2,1,0:T(8,128)}, f32[32,2,16,256]{3,2,1,0:T(8,128)S(1)}, u32[]{:S(2)}, u32[]{:S(2)}) %collective-permute-start.4) | collective-permute-done | bytes 1048608 | tf_op jit(solution)/shard_map/ppermute | solution.py:219
  191.7 0.2 pad_maximum_fusion.4
  191.9 0.1 collective-permute-start.5
  192.0 4.1 %collective-permute-done.5 = f32[64,2,16,256]{3,2,1,0:T(8,128)S(1)} collective-permute-done((f32[64,2,16,256]{3,2,1,0:T(8,128)S(1)}, f32[64,2,16,256]{3,2,1,0:T(8,128)S(1)}, u32[]{:S(2)}, u32[]{:S(2)}) %collective-permute-start.5) | collective-permute-done | bytes 2097184 | tf_op jit(solution)/shard_map/ppermute | solution.py:219
  196.1 2.5 pad_maximum_fusion.1.q_ref
  198.6 16.0 %shard_map.106 = (f32[16,128,128]{2,1,0:T(8,128)}, f32[16,2,16,256]{3,2,1,0:T(8,128)}) custom-call(s32[16,28]{1,0:T(8,128)S(1)} %fusion.1.far, s32[16,28]{1,0:T(8,128)S(1)} %copy-done.2, f32[128,2,16,256]{3,2,1,0:T(8,128)} %pad_maximum_fusion.1.q_ref, f32[316,128,128]{2,1,0:T(8,128)} %bitcast.59, ...), custom_call_target="tpu_custom_call", output_to_operand_aliasing={{0}: (5, {})} | custom-call | tf_op jit(solution)/shard_map/pallas_call | solution.py:135
  214.6 0.0 all-gather.10.cloned.1.call-update
  214.6 0.1 copy.44
  214.7 14.7 %all-gather.8.cloned.1.call-done = f32[64,2,16,256]{3,2,1,0:T(8,128)} async-done(((f32[16,2,16,256]{3,2,1,0:T(8,128)}), f32[64,2,16,256]{3,2,1,0:T(8,128)}) %all-gather.8.cloned.1.call-update) | async-done | bytes 2097168 | tf_op jit(solution)/shard_map/all_gather | solution.py:279
  229.4 46.7 %all-gather.10.cloned.1.call-done = f32[64,2,16,256]{3,2,1,0:T(8,128)} async-done(((f32[16,2,16,256]{3,2,1,0:T(8,128)}), f32[64,2,16,256]{3,2,1,0:T(8,128)}) %all-gather.10.cloned.1.call-update) | async-done | bytes 2097168 | tf_op jit(solution)/shard_map/all_gather | solution.py:279
  276.1 10.3 %shard_map.107 = f32[32,128,128]{2,1,0:T(8,128)} custom-call(s32[32]{0:T(128)S(1)} %get-tuple-element.23.parent, s32[32]{0:T(128)S(1)} %get-tuple-element.22.octant, f32[4,16,2,16,256]{4,3,2,1,0:T(8,128)} %bitcast.68, f32[4,16,2,16,256]{4,3,2,1,0:T(8,128)} %bitcast.69, f32[128,256]{1,0:T(8,128)S(1)} %bitcast.56, f32[256,128]{1,0:T(8,128)S(1)} %bitcast.57, ...), custom_call_target="tpu_custom_call" | custom-call | tf_op jit(solution)/shard_map/pallas_call | solution.py:193
  (16 shorter events, 0.1 us)
Async XLA Ops:
  7.2 33.6 %all-gather.6.cloned.1.call-start = ((), (), s32[]{:S(2)}) async-start(), calls=%async_computation.2 | async-start | bytes 1310720 | tf_op jit(solution)/shard_map/all_gather | solution.py:257
  9.0 96.0 %reduce-scatter.3.cloned.1.call-start = ((), (), s32[]{:S(2)}) async-start(), calls=%async_computation.3 | async-start | bytes 2621440 | tf_op jit(solution)/shard_map/reduce_scatter | solution.py:263
  45.5 1.5 copy-start.1
  61.4 89.3 %reduce-scatter.5.cloned.1.call-start = ((), (), s32[]{:S(2)}) async-start(), calls=%async_computation.4 | async-start | bytes 2621440 | tf_op jit(solution)/shard_map/reduce_scatter | solution.py:263
  62.2 167.2 %all-gather.8.cloned.1.call-start = ((), (), s32[]{:S(2)}) async-start(), calls=%async_computation.5 | async-start | bytes 2621440 | tf_op jit(solution)/shard_map/all_gather | solution.py:279
  104.9 38.9 %copy-start.4 = (f32[32,16,256]{2,1,0:T(8,128)S(1)}, f32[32,16,256]{2,1,0:T(8,128)}, u32[]{:S(2)}) copy-start(f32[32,16,256]{2,1,0:T(8,128)} %reduce-scatter.3.cloned.1.call-done) | copy-start | bytes 1572868
  104.9 13.7 %collective-permute-start = (f32[16,2,16,256]{3,2,1,0:T(8,128)}, f32[16,2,16,256]{3,2,1,0:T(8,128)S(1)}, u32[]{:S(2)}, u32[]{:S(2)}) collective-permute-start(f32[16,2,16,256]{3,2,1,0:T(8,128)} %bitcast.64), channel_id=1, source_target_pairs={{0,16},{4,20},{8,24},{12,28},{16,0},{20,4},{24,8},{28,12},{1,17},{... | collective-permute-start | bytes 1572872 | tf_op jit(solution)/shard_map/ppermute | solution.py:219
  119.8 24.0 %collective-permute-start.1 = (f32[32,2,16,256]{3,2,1,0:T(8,128)S(1)}, f32[32,2,16,256]{3,2,1,0:T(8,128)S(1)}, u32[]{:S(2)}, u32[]{:S(2)}) collective-permute-start(f32[32,2,16,256]{3,2,1,0:T(8,128)S(1)} %pad_maximum_fusion.5), channel_id=1, source_target_pairs={{0,8},{4,12},{8,0},{12,4},{16,24},{20,28},{24,16},{28,20},{1,9},{5... | collective-permute-start | bytes 3145736 | tf_op jit(solution)/shard_map/ppermute | solution.py:219
  144.0 4.2 %collective-permute-start.2 = (f32[64,2,16,256]{3,2,1,0:T(8,128)S(1)}, f32[64,2,16,256]{3,2,1,0:T(8,128)S(1)}, u32[]{:S(2)}, u32[]{:S(2)}) collective-permute-start(f32[64,2,16,256]{3,2,1,0:T(8,128)S(1)} %pad_maximum_fusion.3), channel_id=1, source_target_pairs={{0,4},{4,0},{8,12},{12,8},{16,20},{20,16},{24,28},{28,24},{1,5},{5... | collective-permute-start | bytes 6291464 | tf_op jit(solution)/shard_map/ppermute | solution.py:219
  150.7 17.9 %copy-start.5 = (s32[16,28]{1,0:T(8,128)S(1)}, s32[16,28]{1,0:T(8,128)}, u32[]{:S(2)}) copy-start(s32[16,28]{1,0:T(8,128)} %param.16) | copy-start | bytes 5380
  150.7 17.9 %copy-start = (f32[16,2,8192]{2,1,0:T(2,128)S(1)}, f32[16,2,8192]{2,1,0:T(2,128)}, u32[]{:S(2)}) copy-start(f32[16,2,8192]{2,1,0:T(2,128)} %param.14) | copy-start | bytes 3145732
  150.7 17.9 %copy-start.2 = (s32[16,28]{1,0:T(8,128)S(1)}, s32[16,28]{1,0:T(8,128)}, u32[]{:S(2)}) copy-start(s32[16,28]{1,0:T(8,128)} %kind.3) | copy-start | bytes 5380
  150.7 14.2 %collective-permute-start.3 = (f32[16,2,16,256]{3,2,1,0:T(8,128)}, f32[16,2,16,256]{3,2,1,0:T(8,128)S(1)}, u32[]{:S(2)}, u32[]{:S(2)}) collective-permute-start(f32[16,2,16,256]{3,2,1,0:T(8,128)} %bitcast.60), channel_id=1, source_target_pairs={{0,16},{4,20},{8,24},{12,28},{16,0},{20,4},{24,8},{28,12},{1,17},{... | collective-permute-start | bytes 1572872 | tf_op jit(solution)/shard_map/ppermute | solution.py:219
  167.1 24.6 %collective-permute-start.4 = (f32[32,2,16,256]{3,2,1,0:T(8,128)}, f32[32,2,16,256]{3,2,1,0:T(8,128)S(1)}, u32[]{:S(2)}, u32[]{:S(2)}) collective-permute-start(f32[32,2,16,256]{3,2,1,0:T(8,128)} %pad_maximum_fusion.6), channel_id=1, source_target_pairs={{0,8},{4,12},{8,0},{12,4},{16,24},{20,28},{24,16},{28,20},{1,9},{5... | collective-permute-start | bytes 3145736 | tf_op jit(solution)/shard_map/ppermute | solution.py:219
  168.6 23.1 %copy-start.3 = (f32[32,16,256]{2,1,0:T(8,128)S(1)}, f32[32,16,256]{2,1,0:T(8,128)}, u32[]{:S(2)}) copy-start(f32[32,16,256]{2,1,0:T(8,128)} %reduce-scatter.5.cloned.1.call-done) | copy-start | bytes 1572868
  184.6 91.5 %all-gather.10.cloned.1.call-start = ((), (), s32[]{:S(2)}) async-start(), calls=%async_computation.6 | async-start | bytes 2621440 | tf_op jit(solution)/shard_map/all_gather | solution.py:279
  191.9 4.2 %collective-permute-start.5 = (f32[64,2,16,256]{3,2,1,0:T(8,128)S(1)}, f32[64,2,16,256]{3,2,1,0:T(8,128)S(1)}, u32[]{:S(2)}, u32[]{:S(2)}) collective-permute-start(f32[64,2,16,256]{3,2,1,0:T(8,128)S(1)} %pad_maximum_fusion.4), channel_id=1, source_target_pairs={{0,4},{4,0},{8,12},{12,8},{16,20},{20,16},{24,28},{28,24},{1,5},{5... | collective-permute-start | bytes 6291464 | tf_op jit(solution)/shard_map/ppermute | solution.py:219
Sparse Core Ops, SparseCore 0:
  10.1 30.6 all-gather.5
  61.5 43.3 reduce-scatter.2
  107.3 43.1 reduce-scatter.4
  184.8 44.5 all-gather.7
  231.4 44.6 all-gather.9
where the time goes:
time: 296 us; the launch traced here: 293 us
  waiting for transfers between devices  197 us (67%)
  Pallas kernels  56.7 us (19%)
  between operations  13.9 us (5%)
  other arithmetic  11.9 us (4%)
  local copies, waits for them, and re-layouts  6.77 us (2%)
  starting transfers between devices  6.37 us (2%)
    ppermute x6, waiting for transfers between devices, gather_box(): other = lax.ppermute(x, 'box', [(i, i ^ 1 << bit) for i in range(nb)])  62.7 us
    all_gather x2, waiting for transfers between devices, shards(): incoming.append(lax.all_gather(planes, 'dir', axis=0))  61.4 us
    reduce_scatter x2, waiting for transfers between devices, shards(): lax.psum_scatter(partial.reshape((nd * parents * 2,) + partial.shape[3:])...  42.7 us
    pallas_call x2, Pallas kernels, translate(): pl.pallas_call(functools.partial(translate_kernel, chunk), grid_spec=pltp...  31.9 us
    all_gather x1, waiting for transfers between devices, shards(): phases = lax.all_gather(shift_phase.reshape(8, tl, pc), 'dir', axis=0)  29.7 us
    pallas_call x1, Pallas kernels, gather_up(): pl.pallas_call(functools.partial(gather_up_kernel, group), grid_spec=pltp...  14.4 us
    pallas_call x1, Pallas kernels, spread_down(): pl.pallas_call(functools.partial(spread_down_kernel, group), grid_spec=pl...  10.3 us
    concatenate x6, other arithmetic, gather_box(): x = jnp.concatenate([x, other], axis=0)  8.62 us
  transfers between devices with their start and end apart: 11, of which 10 were waited for; matrix products, arithmetic and copies ran while one was open for 3% of the time, Pallas kernels for 11%

commit v1 on v0

v1 whole, which is shorter than its diff:
```python
import functools

import jax
import jax.numpy as jnp
from jax import lax
from jax.experimental import pallas as pl
from jax.experimental.pallas import tpu as pltpu
from jax.sharding import PartitionSpec as P

F32, BF16, I32 = jnp.float32, jnp.bfloat16, jnp.int32
MESH = pl.DeviceIdType.MESH
VMEM_BYTES = 60 * 1024 * 1024
ROWS = 8
GROUP = 4
OCT = 8

COS = (
    0.999999999880854,
    -0.49999999845758136,
    0.04166666339221376,
    -0.001388886238622854,
    2.48005323812661e-05,
    -2.753445728365435e-07,
    2.0600835499376906e-09,
    -9.713911649043148e-12,
)
SIN = (
    0.9999999992304494,
    -0.166666659035747,
    0.008333320978968734,
    -0.00019840518737424315,
    2.7535517055355563e-06,
    -2.4725519533129986e-08,
    1.360099414116501e-10,
)


def split(x):
    hi = x.astype(BF16)
    return hi, (x - hi.astype(F32)).astype(BF16)


def dot3(a, b):
    (ah, al), (bh, bl) = a, b
    d = functools.partial(jnp.dot, preferred_element_type=F32)
    return d(ah, bh) + (d(ah, bl) + d(al, bh))


def horner(y, coefficients):
    r = jnp.full_like(y, coefficients[-1])
    for c in coefficients[-2::-1]:
        r = r * y + c
    return r


def rows_view(x):
    n, _, k = x.shape
    return x.reshape(n, 2, k // 128, 128).transpose(0, 2, 1, 3).reshape(n, k // 64, 128)


def rows_unview(x):
    n, r, _ = x.shape
    return x.reshape(n, r // 2, 2, 128).transpose(0, 2, 1, 3).reshape(n, 2, r * 64)


def neighbours(v):
    return pltpu.roll(v, 7, v.ndim - 2), pltpu.roll(v, 1, v.ndim - 2)


def even_rows(shape):
    return lax.broadcasted_iota(I32, shape, len(shape) - 2) % 2 == 0


def kernel(
    dims,
    itab,
    ftab,
    far_ref,
    phase_ref,
    x_ref,
    phi_ref,
    theta_ref,
    thetat_ref,
    phit_ref,
    upper_ref,
    trans_ref,
    coarse_ref,
    fine_ref,
    trans,
    farr,
    fars,
    zp,
    pf,
    cc,
    cs,
    alh,
    all_,
    th,
    tl_,
    tth,
    ttl,
    wide,
    widet,
    mask,
    maskt,
    sb,
    part,
    ar,
    qa,
    ql,
    qs,
    ts,
    ta,
    cg,
    xl,
    kl,
    fa,
    sem_tr,
    sem_fs,
    far_s,
    far_r,
    zp_s,
    zp_r,
    pf_s,
    pf_r,
    up_s,
    up_r,
    q_s,
    q_r,
    t_s,
    t_r,
    dr_s,
    dl_s,
    d_r,
):
    nb, nd, C, n, parents, many, bits = dims
    R = nd * GROUP * 8
    b, z = lax.axis_index("box"), lax.axis_index("dir")
    g, h = b % GROUP, b // GROUP
    pr = OCT * 16 // nb
    PERM, OCTS, PARENT, OCTANT, LAST = (i * n for i in range(5))

    def remote(src, dst, ss, rs, dev):
        return pltpu.make_async_remote_copy(
            src_ref=src, dst_ref=dst, send_sem=ss, recv_sem=rs, device_id=dev, device_id_type=MESH
        )

    def zp_copy(c, j):
        to = (z + j) % nd
        return remote(
            phase_ref.at[c, pl.ds(pl.multiple_of(b * pr, 8), pr)],
            zp.at[c, z],
            zp_s.at[c, j],
            zp_r.at[c, j],
            (b, to),
        )

    def pf_copy(c, j):
        return remote(zp.at[c], pf.at[c, b], pf_s.at[c, j], pf_r.at[c, j], (b ^ j, z))

    def far_copy(j):
        return remote(far_ref, farr.at[g], far_s.at[j], far_r.at[j], (b ^ j, z))

    def right_copy(c, d):
        return remote(part.at[c, d], ar.at[c, d], up_s.at[c, d], up_r.at[c, d], (b, z + 1))

    def left_copy(c, d):
        slot = jnp.where(z - 1 == d, nd, d)
        return remote(part.at[c, d], ar.at[c, slot], up_s.at[c, d], up_r.at[c, slot], (b, z - 1))

    def up_wait(c, slot):
        return remote(part.at[c, 0], ar.at[c, slot], up_s.at[c, 0], up_r.at[c, slot], (b, z))

    def q_copy(c, j):
        to = b ^ j
        return remote(
            part.at[c, z, to % GROUP], qa.at[c, b], q_s.at[c, j], q_r.at[c, j], (to, z)
        )

    def t_copy(c, j):
        return remote(ts.at[c, g ^ j], ta.at[c, g], t_s.at[c, j], t_r.at[c, j], (b ^ j, z))

    def down_right(c, d):
        return remote(cg.at[c, d], cg.at[c, d], dr_s.at[c, d], d_r.at[c, d], (b, z + 1))

    def down_left(c, d):
        return remote(cg.at[c, d], cg.at[c, d], dl_s.at[c, d], d_r.at[c, d], (b, z - 1))

    def trans_copy(c):
        row = pl.multiple_of((c * GROUP + g) * 8, 8)
        return pltpu.make_async_copy(trans_ref.at[:, pl.ds(row, 8)], trans.at[c], sem_tr.at[c])

    for c in range(C):
        trans_copy(c).start()

    barrier = pltpu.get_barrier_semaphore()
    for j in range(1, nb):
        pl.semaphore_signal(barrier, inc=1, device_id=(b ^ j, z), device_id_type=MESH)
    for j in range(1, nd):
        pl.semaphore_signal(barrier, inc=1, device_id=(b, (z + j) % nd), device_id_type=MESH)
    pl.semaphore_wait(barrier, nb + nd - 2)

    for c in range(C):
        for j in range(1, nd):
            zp_copy(c, j).start()
    for j in range(1, GROUP):
        far_copy(j).start()
    for c in range(C):
        zp[c, z] = phase_ref[c, pl.ds(pl.multiple_of(b * pr, 8), pr), :]
    farr[g] = far_ref[...]

    phi = split(phi_ref[...])
    many_children = 4

    def along(i, _):
        rows = x_ref.shape[1]
        v = x_ref[pl.ds(i * many_children, many_children)].reshape(many_children * rows, 128)
        y = dot3(split(v), phi)
        for q in range(many_children):
            for half in range(2):
                hi, lo = split(y[q * rows : (q + 1) * rows, half * 128 : (half + 1) * 128])
                alh[i * many_children + q, half * rows : (half + 1) * rows, :] = hi
                all_[i * many_children + q, half * rows : (half + 1) * rows, :] = lo
        return 0

    def phases_on(c):
        for j in range(1, nd):
            zp_copy(c, j).wait_recv()
        for j in range(1, nb):
            pf_copy(c, j).start()
        pf[c, b] = zp[c]

    def shifts(c):
        for j in range(1, nb):
            pf_copy(c, j).wait_recv()
        per = 16 // pr

        def body(o, _):
            for d in range(nd):
                for j in range(per):
                    v = pf[c, o * per + j, d]
                    y = v * v
                    co, si = horner(y, COS), v * horner(y, SIN)
                    for p in range(2):
                        where = pl.ds(d * 32 + 2 * j * pr + p, pr, stride=2)
                        cc[c, o, where, :] = co
                        cs[c, o, where, :] = si
            return 0

        lax.fori_loop(0, OCT, body, 0)

    tc, tf = theta_ref.shape
    tl = tc // nd

    def axis(shape, d):
        return lax.broadcasted_iota(I32, shape, d)

    def ones(shape, hit):
        return jnp.where(hit, 1.0, 0.0).astype(BF16)

    def fine_row(i):
        return (i >> 1) & (tf - 1)

    def polar_row(c, r):
        r = r & (R - 1)
        return (r >> 5) * tl + c * ROWS + ((r >> 2) & (ROWS - 1))

    def masks():
        shape = (2 * R, 4 * tf)
        r, k = axis(shape, 0), axis(shape, 1)
        p, plane, turned = r & 1, k & 1, r >= R
        same_half = ((r >> 1) & 1) == jnp.where(k >= 2 * tf, 1, 0)
        sign = jnp.where(turned & (p == 0), -1.0, 1.0)
        hit = same_half & ((p != plane) == turned)
        mask[...] = jnp.where(hit, sign, 0.0).astype(BF16)
        shape = (4 * tf, R)
        k, r = axis(shape, 0), axis(shape, 1)
        hit = (((r >> 1) & 1) == jnp.where(k >= 2 * tf, 1, 0)) & ((r & 1) == (k & 1))
        maskt[...] = ones(shape, hit)
        shape = (tf, 4 * tf)
        w = ones(shape, fine_row(axis(shape, 1)) == axis(shape, 0))
        shape = (4 * tf, tf)
        wt = ones(shape, fine_row(axis(shape, 0)) == axis(shape, 1))
        for v, out in zip(split(theta_ref[...]), (0, 1)):
            wide[out] = d32(v, w).astype(BF16)
        for v, out in zip(split(thetat_ref[...]), (0, 1)):
            widet[out] = d32(wt, v).astype(BF16)

    d32 = functools.partial(jnp.dot, preferred_element_type=F32)

    def spread_map(c):
        shape = (2 * R, tc)
        pick = ones(shape, polar_row(c, axis(shape, 0)) == axis(shape, 1))
        for i, out in enumerate((th, tl_)):
            out[...] = d32(pick, wide[i]).astype(BF16) * mask[...]

    def spread_map_back(c):
        shape = (tc, R)
        pick = ones(shape, polar_row(c, axis(shape, 1)) == axis(shape, 0))
        for i, out in enumerate((tth, ttl)):
            out[...] = d32(widet[i], pick).astype(BF16) * maskt[...]

    def aggregate(c):
        spread_map(c)

        def body(kk, acc):
            k = 2 * kk
            i0, i1 = itab[PERM + k], itab[PERM + k + 1]
            rh = jnp.concatenate([alh[i0], alh[i1]], axis=1)
            rl = jnp.concatenate([all_[i0], all_[i1]], axis=1)
            v = dot3((th[...], tl_[...]), (rh, rl))
            for q in range(2):
                o = itab[OCTS + k + q]
                lanes = slice(q * 128, (q + 1) * 128)
                y = cc[c, o] * v[:R, lanes] + cs[c, o] * v[R:, lanes]
                acc = acc * ftab[k + q] + y
                sb[k + q] = acc
            return acc

        lax.fori_loop(0, n // 2, body, jnp.zeros((R, 128), F32))

        def pick(p, _):
            v = sb[itab[LAST + p]] * ftab[n + p]
            part[c, :, :, p] = v.reshape(nd, GROUP, 8, 128)
            return 0

        lax.fori_loop(0, parents, pick, 0)

    def add(c, d, slot):
        def body(k, _):
            part[c, d, k] = part[c, d, k] + ar[c, slot, k]
            return 0

        lax.fori_loop(0, GROUP, body, 0)

    def send_ends(c):
        @pl.when(z == 0)
        def _():
            for d in range(nd - 1, 0, -1):
                right_copy(c, d).start()

        @pl.when(z == nd - 1)
        def _():
            for d in range(nd - 1):
                left_copy(c, d).start()

    def hop(c, k):
        d = nd - 1 - k

        @pl.when(jnp.logical_and(z < d, z > 0))
        def _():
            up_wait(c, d).wait_recv()
            add(c, d, d)
            right_copy(c, d).start()

        @pl.when(jnp.logical_and(z > k, z < nd - 1))
        def _():
            up_wait(c, k).wait_recv()
            add(c, k, k)
            left_copy(c, k).start()

    def finish_up(c):
        @pl.when(z > 0)
        def _():
            up_wait(c, z).wait_recv()
            add(c, z, z)

        @pl.when(z < nd - 1)
        def _():
            up_wait(c, nd).wait_recv()
            add(c, z, nd)

        for j in range(1, nb):
            q_copy(c, j).start()
        qa[c, b] = part[c, z, g]

    def translate(c):
        if c == 0:
            for j in range(1, GROUP):
                far_copy(j).wait_recv()
            move = pltpu.make_async_copy(farr, fars, sem_fs)
            move.start()
            move.wait()
            for i in range(C):
                trans_copy(i).wait()
        for j in range(1, nb):
            q_copy(c, j).wait_recv()

        def stage(s, _):
            v = qa[c, s]
            below, above = neighbours(v)
            ql[pl.ds(s * parents, parents)] = v
            qs[pl.ds(s * parents, parents)] = jnp.where(even_rows(v.shape), below, above)
            return 0

        lax.fori_loop(0, nb, stage, 0)
        even = even_rows((8, 128))
        for jg in range(GROUP):

            def body(p, _):
                u = w = None
                for l in range(many):
                    code = fars[jg, p, l]
                    f, kind = code & ((1 << bits) - 1), code >> bits
                    a = trans[c, kind]
                    r, i = a * ql[f], a * qs[f]
                    u = r if u is None else u + r
                    w = i if w is None else w + i
                re = u - pltpu.roll(u, 7, 0)
                im = w + pltpu.roll(w, 1, 0)
                ts[c, jg, p] = jnp.where(even, re, im)
                return 0

            lax.fori_loop(0, parents, body, 0)
        for j in range(1, GROUP):
            t_copy(c, j).start()
        ta[c, g] = ts[c, g]

    def coarse(c):
        for j in range(1, GROUP):
            t_copy(c, j).wait_recv()

        def body(p, _):
            rows = pl.ds(c * GROUP * 8, GROUP * 8)
            v = ta[c, :, p] + upper_ref[p, rows, :].reshape(GROUP, 8, 128)
            coarse_ref[p, rows, :] = v.reshape(GROUP * 8, 128)
            cg[c, z, :, p] = v
            return 0

        lax.fori_loop(0, parents, body, 0)

        @pl.when(z < nd - 1)
        def _():
            down_right(c, z).start()

        @pl.when(z > 0)
        def _():
            down_left(c, z).start()

    def pass_down(c, k):
        @pl.when(z >= k)
        def _():
            down_right(c, z - k).wait_recv()

            @pl.when(z < nd - 1)
            def _():
                down_right(c, z - k).start()

        @pl.when(z + k < nd)
        def _():
            down_left(c, z + k).wait_recv()

            @pl.when(z > 0)
            def _():
                down_left(c, z + k).start()

    def disaggregate(c):
        spread_map_back(c)

        def stage(p, _):
            v = cg[c, :, :, p].reshape(nd * GROUP, 8, 128)
            below, above = neighbours(v)
            xl[p] = v.reshape(R, 128)
            kl[p] = jnp.where(even_rows(v.shape), below, -above).reshape(R, 128)
            return 0

        lax.fori_loop(0, parents, stage, 0)
        phit = split(phit_ref[...]) if c == C - 1 else None

        def body(ii, _):
            ys = []
            for q in range(2):
                p, o = itab[PARENT + 2 * ii + q], itab[OCTANT + 2 * ii + q]
                ys.append(cc[c, o] * xl[p] + cs[c, o] * kl[p])
            v = dot3((tth[...], ttl[...]), split(jnp.concatenate(ys, axis=1)))
            for q in range(2):
                w = v[:, q * 128 : (q + 1) * 128]
                if c > 0:
                    w = w + fa[2 * ii + q]
                if c < C - 1:
                    fa[2 * ii + q] = w
                else:
                    half = w.shape[0] // 2
                    line = jnp.concatenate([w[:half], w[half:]], axis=1)
                    fine_ref[2 * ii + q] = dot3(split(line), phit)
            return 0

        lax.fori_loop(0, n // 2, body, 0)

    masks()
    lax.fori_loop(0, n // many_children, along, 0)
    for c in range(C):
        phases_on(c)
    shifts(0)
    aggregate(0)
    send_ends(0)
    for s in range(C):
        if s + 1 < C:
            shifts(s + 1)
            aggregate(s + 1)
            send_ends(s + 1)
        if s >= 1:
            translate(s - 1)
        if s >= 2:
            for k in range(2, nd):
                pass_down(s - 2, k)
        hop(s, 0)
        if s >= 1:
            coarse(s - 1)
        for k in range(1, nd - 1):
            hop(s, k)
        if s >= 2:
            disaggregate(s - 2)
        finish_up(s)
        if s >= 1:
            pass_down(s - 1, 1)
    translate(C - 1)
    coarse(C - 1)
    if C >= 2:
        for k in range(2, nd):
            pass_down(C - 2, k)
        disaggregate(C - 2)
    for k in range(1, nd):
        pass_down(C - 1, k)
    disaggregate(C - 1)

    for j in range(1, GROUP):
        far_copy(j).wait_send()

    def drain(c, _):
        for j in range(1, nd):
            zp_copy(c, j).wait_send()
        for j in range(1, nb):
            pf_copy(c, j).wait_send()
            q_copy(c, j).wait_send()
        for j in range(1, GROUP):
            t_copy(c, j).wait_send()
        for d in range(nd):

            @pl.when(d > z)
            def _():
                right_copy(c, d).wait_send()

            @pl.when(d < z)
            def _():
                left_copy(c, d).wait_send()

            @pl.when(jnp.logical_and(d <= z, z < nd - 1))
            def _():
                down_right(c, d).wait_send()

            @pl.when(jnp.logical_and(d >= z, z > 0))
            def _():
                down_left(c, d).wait_send()

        return 0

    lax.fori_loop(0, C, drain, 0)


def shards(
    fine_out,
    theta_interp,
    phi_interp,
    shift_phase,
    translation,
    upper_in,
    children,
    far_boxes,
    far_offsets,
):
    n = fine_out.shape[0]
    tc, tf = theta_interp.shape
    pf_, pc = phi_interp.shape
    parents, many = far_boxes.shape
    nb, nd = lax.axis_size("box"), lax.axis_size("dir")
    noff = translation.shape[0]
    tl = tc // nd
    C = tl // ROWS
    R = nd * GROUP * 8
    bits = (nb * parents - 1).bit_length()

    flat = (children % (n * nd)).reshape(-1)
    own = lax.axis_index("dir") * n + jnp.arange(n, dtype=I32)
    slots = jnp.arange(flat.shape[0], dtype=I32)
    ids = jnp.arange(n, dtype=I32)
    slot = jnp.sum(jnp.where(flat[None, :] == own[:, None], slots[None, :], 0), axis=1)
    before = slot[None, :] < slot[:, None]
    rank = jnp.sum(before.astype(I32), axis=1)
    parent, octant = slot // OCT, slot % OCT
    same = jnp.any(before & (parent[None, :] == parent[:, None]), axis=1).astype(I32)
    at = rank[None, :] == ids[:, None]
    packed = jnp.sum(jnp.where(at, (ids * OCT + octant)[None, :] * 2 + same[None, :], 0), axis=1)
    boxes = jnp.arange(parents, dtype=I32)
    upto = jnp.sum((parent[None, :] <= boxes[:, None]).astype(I32), axis=1)
    has = jnp.any(parent[None, :] == boxes[:, None], axis=1)
    itab = jnp.concatenate(
        [packed // (2 * OCT), packed // 2 % OCT, parent, octant, jnp.maximum(upto - 1, 0)]
    )
    ftab = jnp.concatenate([(packed % 2).astype(F32), has.astype(F32)])
    far = jnp.pad(far_boxes + (far_offsets << bits), ((0, 0), (0, 128 - many)))

    phases = (
        shift_phase.reshape(OCT, C, ROWS * 2, 128).transpose(1, 0, 2, 3).reshape(C, OCT * 16, 128)
    )

    vmem, smem, hbm = (
        pl.BlockSpec(memory_space=m) for m in (pltpu.VMEM, pltpu.SMEM, pl.ANY)
    )
    dma = pltpu.SemaphoreType.DMA
    tile = (GROUP, parents, 8, 128)
    rows, fine_rows = C * GROUP * 8, tf * 2
    coarse_in, fine_in = pl.pallas_call(
        functools.partial(kernel, (nb, nd, C, n, parents, many, bits)),
        in_specs=[smem, smem] + [vmem] * 8 + [hbm],
        out_specs=[vmem, vmem],
        out_shape=[
            jax.ShapeDtypeStruct((parents, rows, 128), F32),
            jax.ShapeDtypeStruct((n, fine_rows, pf_), F32),
        ],
        scratch_shapes=[
            pltpu.VMEM((C, noff, 8, 128), F32),
            pltpu.VMEM((GROUP, parents, 128), I32),
            pltpu.SMEM((GROUP, parents, 128), I32),
            pltpu.VMEM((C, nd, OCT * 16 // nb, 128), F32),
            pltpu.VMEM((C, nb, nd, OCT * 16 // nb, 128), F32),
            pltpu.VMEM((C, OCT, R, 128), F32),
            pltpu.VMEM((C, OCT, R, 128), F32),
            pltpu.VMEM((n, 2 * fine_rows, 128), BF16),
            pltpu.VMEM((n, 2 * fine_rows, 128), BF16),
            pltpu.VMEM((2 * R, 4 * tf), BF16),
            pltpu.VMEM((2 * R, 4 * tf), BF16),
            pltpu.VMEM((4 * tf, R), BF16),
            pltpu.VMEM((4 * tf, R), BF16),
            pltpu.VMEM((2, tc, 4 * tf), BF16),
            pltpu.VMEM((2, 4 * tf, tc), BF16),
            pltpu.VMEM((2 * R, 4 * tf), BF16),
            pltpu.VMEM((4 * tf, R), BF16),
            pltpu.VMEM((n, R, 128), F32),
            pltpu.VMEM((C, nd) + tile, F32),
            pltpu.VMEM((C, nd + 1) + tile, F32),
            pltpu.VMEM((C, nb) + tile[1:], F32),
            pltpu.VMEM((nb * parents, 8, 128), F32),
            pltpu.VMEM((nb * parents, 8, 128), F32),
            pltpu.VMEM((C,) + tile, F32),
            pltpu.VMEM((C,) + tile, F32),
            pltpu.VMEM((C, nd) + tile, F32),
            pltpu.VMEM((parents, R, 128), F32),
            pltpu.VMEM((parents, R, 128), F32),
            pltpu.VMEM((n, 4 * tf, 128), F32),
            dma((C,)),
            dma,
            dma((GROUP,)),
            dma((GROUP,)),
            dma((C, nd)),
            dma((C, nd)),
            dma((C, nb)),
            dma((C, nb)),
            dma((C, nd)),
            dma((C, nd + 1)),
            dma((C, nb)),
            dma((C, nb)),
            dma((C, GROUP)),
            dma((C, GROUP)),
            dma((C, nd)),
            dma((C, nd)),
            dma((C, nd)),
        ],
        compiler_params=pltpu.CompilerParams(
            collective_id=0, has_side_effects=True, vmem_limit_bytes=VMEM_BYTES
        ),
    )(
        itab,
        ftab,
        far,
        phases,
        rows_view(fine_out),
        phi_interp,
        theta_interp,
        theta_interp.T,
        phi_interp.T,
        rows_view(upper_in),
        rows_view(translation),
    )
    return rows_unview(coarse_in), rows_unview(fine_in)


def solution(mesh):
    placed = (
        P(("box", "dir"), None, None),
        P(),
        P(),
        P(None, "dir"),
        P(None, None, "dir"),
        P("box", None, "dir"),
        P("box", None),
        P("box", None),
        P("box", None),
    )
    return jax.shard_map(
        shards,
        mesh=mesh,
        in_specs=placed,
        out_specs=(P("box", None, "dir"), P(("box", "dir"), None, None)),
        check_vma=False,
    )
```

time: 296 us -> 236 us (0.80); the launches traced: 293 us -> 236 us
  waiting for transfers between devices: 197 us -> 0 us
  Pallas kernels: 56.7 us -> 222 us
  between operations: 13.9 us -> 0.71 us
  other arithmetic: 11.9 us -> 3.01 us
  starting transfers between devices: 6.37 us -> 0 us
  local copies, waits for them, and re-layouts: 6.77 us -> 10 us
    pallas_call x4 -> x1, Pallas kernels: 56.7 us -> 222 us  [shards(): pl.pallas_call(functools.partial(kernel, (nb, nd, C, n, parents, many, bi...]
    all_gather x3 -> x0, waiting for transfers between devices: 91.1 us -> none  [the longest x2 61.4 us: shards(): incoming.append(lax.all_gather(planes, 'dir', axis=0))]
    ppermute x6 -> x0, waiting for transfers between devices: 62.7 us -> none  [gather_box(): other = lax.ppermute(x, 'box', [(i, i ^ 1 << bit) for i in range(nb)])]
    reduce_scatter x2 -> x0, waiting for transfers between devices: 42.7 us -> none  [shards(): lax.psum_scatter(partial.reshape((nd * parents * 2,) + partial.shape[3:])...]
    concatenate x6 -> x1, other arithmetic: 8.62 us -> 0.66 us  [shards(): ftab = jnp.concatenate([(packed % 2).astype(F32), has.astype(F32)])]
    ppermute x6 -> x0, starting transfers between devices: 6.17 us -> none  [gather_box(): other = lax.ppermute(x, 'box', [(i, i ^ 1 << bit) for i in range(nb)])]
    unnamed x15 -> x6, local copies, waits for them, and re-layouts: 1.86 us -> 6.9 us
    another operation x1 -> x0, local copies, waits for them, and re-layouts: 4.66 us -> none  [shards(): cs = jnp.stack([jnp.cos(phases), jnp.sin(phases)], axis=1)]
  transfers between devices with their start and end apart: 11 -> 0, of which waited for: 10 -> 0; matrix products, arithmetic and copies ran while one was open for 3% -> 0% of each run, Pallas kernels for 11% -> 0%
where the time goes in v1:
time: 236 us
  Pallas kernels  222 us (94%)
  local copies, waits for them, and re-layouts  10 us (4%)
  other arithmetic  3.01 us (1%)
    pallas_call x1, Pallas kernels, shards(): pl.pallas_call(functools.partial(kernel, (nb, nd, C, n, parents, many, bi...  222 us
    unnamed x6, local copies, waits for them, and re-layouts  6.9 us

profile of v1, /device:TPU:0, one launch (start us, length us, event | category | flops | bytes accessed | tf_op | source)
XLA Modules:
  0.0 235.9 jit_solution(14367314928027917634)
XLA Ops:
  0.6 0.7 add_select_fusion
  1.3 0.1 copy.29
  1.4 0.1 eq.28
  1.5 0.2 select_reduce_fusion.1
  1.7 0.1 fusion.2
  1.8 0.1 convert_reduce_fusion
  2.0 0.2 fusion.1
  2.1 0.2 fusion
  2.3 0.1 select_reduce_fusion
  2.5 0.7 concatenate.6.itab
  3.1 0.7 pad_maximum_fusion.ftab
  3.8 0.7 shift-left_add_fusion
  4.5 0.6 pad.4.far_ref
  5.1 1.5 copy.35.theta_ref
  6.6 1.7 copy.32
  8.3 1.7 copy.30
  10.0 222.2 %shard_map.104 = (f32[16,128,128]{2,1,0:T(8,128)}, f32[32,128,128]{2,1,0:T(8,128)}) custom-call(s32[144]{0:T(256)} %concatenate.6.itab, f32[48]{0:T(128)} %pad_maximum_fusion.ftab, s32[16,128]{1,0:T(8,128)} %pad.4.far_ref, f32[4,128,128]{2,1,0:T(8,128)} %bitcast.34, f32[32,128,128]{2,1,0:T(8,128)} %bitcast.32, f32[128,256]{1,0:T(8,128)} %phi_ref.1, ...), custom_call_target="tpu_custom_call" | custom-call | tf_op jit(solution)/shard_map/pallas_call | solution.py:613
  232.2 0.0 copy-start
  232.2 2.4 %copy.40 = f32[16,2,8192]{2,1,0:T(2,128)} copy(f32[16,2,8192]{2,1,0:T(2,128)} %bitcast.36) | data formatting | bytes 2097152
  234.6 0.0 copy-done
  234.6 1.3 copy.41
  (6 shorter events, 0.1 us)
Async XLA Ops:
  232.2 2.5 %copy-start = (f32[32,128,128]{2,1,0:T(8,128)S(1)}, f32[32,128,128]{2,1,0:T(8,128)}, u32[]{:S(2)}) copy-start(f32[32,128,128]{2,1,0:T(8,128)} %get-tuple-element.5) | copy-start | bytes 6291460

commit v2 on v1

--- a/solution.py
+++ b/solution.py
@@ -10,8 +10,11 @@
 F32, BF16, I32 = jnp.float32, jnp.bfloat16, jnp.int32
 MESH = pl.DeviceIdType.MESH
 VMEM_BYTES = 60 * 1024 * 1024
-ROWS = 8
-GROUP = 4
+FINE = 2
+ORDERS = {
+    (4, 8): (0, 0, 0, 0, 1, 0, 3, 1, 1, 0, 3, 1, 3, 5, 1, 2, 1, 2, 3, 2, 0, 2, 3, 1, 0, 2, 3, 1, 2, 5, 3, 0, 1, 5, 2, 4, 0, 5, 5, 2, 4, 0, 4, 1, 7, 4, 2, 3, 4, 5, 0, 3, 6, 4, 5, 6, 1, 7, 6, 3, 4, 6, 7, 6, 7, 5, 3, 2, 7, 1, 6, 3, 2, 4, 6, 7, 2, 5, 7, 4, 6, 5, 6, 7, 5, 4, 6, 7, 5, 6, 4, 7, 6, 4, 7, 7),
+    (4, 4): (2, 2, 0, 0, 2, 0, 1, 2, 0, 1, 0, 2, 0, 2, 3, 0, 1, 3, 1, 1, 2, 0, 3, 1, 3, 2, 3, 0, 2, 1, 3, 1, 0, 1, 3, 2, 0, 3, 1, 2, 3, 1, 0, 2, 3, 1, 3, 3),
+}
 OCT = 8
 
 COS = (
@@ -40,9 +43,10 @@
     return hi, (x - hi.astype(F32)).astype(BF16)
 
 
-def dot3(a, b):
+def dot3(a, b, turned=False):
     (ah, al), (bh, bl) = a, b
-    d = functools.partial(jnp.dot, preferred_element_type=F32)
+    sums = (((1,), (1 if turned else 0,)), ((), ()))
+    d = functools.partial(lax.dot_general, dimension_numbers=sums, preferred_element_type=F32)
     return d(ah, bh) + (d(ah, bl) + d(al, bh))
 
 
@@ -53,6 +57,10 @@
     return r
 
 
+def pair_of(rows, chunks):
+    return 2 if rows <= 64 and chunks % 2 == 0 else 1
+
+
 def rows_view(x):
     n, _, k = x.shape
     return x.reshape(n, 2, k // 128, 128).transpose(0, 2, 1, 3).reshape(n, k // 64, 128)
@@ -73,20 +81,20 @@
 
 def kernel(
     dims,
-    itab,
-    ftab,
-    far_ref,
+    children_ref,
+    boxes_ref,
+    kinds_ref,
     phase_ref,
     x_ref,
     phi_ref,
-    theta_ref,
     thetat_ref,
-    phit_ref,
     upper_ref,
     trans_ref,
     coarse_ref,
     fine_ref,
     trans,
+    tabv,
+    itab,
     farr,
     fars,
     zp,
@@ -98,7 +106,6 @@
     th,
     tl_,
     tth,
-    ttl,
     wide,
     widet,
     mask,
@@ -108,7 +115,6 @@
     ar,
     qa,
     ql,
-    qs,
     ts,
     ta,
     cg,
@@ -117,6 +123,7 @@
     fa,
     sem_tr,
     sem_fs,
+    sem_tab,
     far_s,
     far_r,
     zp_s,
@@ -133,12 +140,15 @@
     dl_s,
     d_r,
 ):
-    nb, nd, C, n, parents, many, bits = dims
-    R = nd * GROUP * 8
+    nb, nd, C, ROWS, n, parents, many, bits = dims
+    GROUP = ROWS // 2
+    PER = GROUP * 8
+    R = nd * PER
+    PAIR = pair_of(R, C)
     b, z = lax.axis_index("box"), lax.axis_index("dir")
     g, h = b % GROUP, b // GROUP
-    pr = OCT * 16 // nb
-    PERM, OCTS, PARENT, OCTANT, LAST = (i * n for i in range(5))
+    pr = OCT * 2 * ROWS // nb
+    PERM, OCTS, PARENT, OCTANT, LAST, KEEP, HAS = range(7)
 
     def remote(src, dst, ss, rs, dev):
         return pltpu.make_async_remote_copy(
@@ -159,7 +169,7 @@
         return remote(zp.at[c], pf.at[c, b], pf_s.at[c, j], pf_r.at[c, j], (b ^ j, z))
 
     def far_copy(j):
-        return remote(far_ref, farr.at[g], far_s.at[j], far_r.at[j], (b ^ j, z))
+        return remote(farr.at[g], farr.at[g], far_s.at[j], far_r.at[j], (b ^ j, z))
 
     def right_copy(c, d):
         return remote(part.at[c, d], ar.at[c, d], up_s.at[c, d], up_r.at[c, d], (b, z + 1))
@@ -193,6 +203,7 @@
     for c in range(C):
         trans_copy(c).start()
 
+    farr[g, :, 0:many] = boxes_ref[...] + (kinds_ref[...] << bits)
     barrier = pltpu.get_barrier_semaphore()
     for j in range(1, nb):
         pl.semaphore_signal(barrier, inc=1, device_id=(b ^ j, z), device_id_type=MESH)
@@ -207,7 +218,33 @@
         far_copy(j).start()
     for c in range(C):
         zp[c, z] = phase_ref[c, pl.ds(pl.multiple_of(b * pr, 8), pr), :]
-    farr[g] = far_ref[...]
+
+    lanes = lax.broadcasted_iota(I32, (1, 128), 1)
+
+    def table(p, carry):
+        k, rows = carry[0], list(carry[1:])
+        first = k
+        for o in range(OCT):
+            local = lax.rem(children_ref[o, p], n * nd) - z * n
+            own = jnp.logical_and(local >= 0, local < n)
+            here, at = lanes == jnp.where(own, k, -1), lanes == jnp.where(own, local, -1)
+            rows[PERM] = jnp.where(here, local, rows[PERM])
+            rows[OCTS] = jnp.where(here, o, rows[OCTS])
+            rows[KEEP] = jnp.where(here, jnp.where(k > first, 1, 0), rows[KEEP])
+            rows[PARENT] = jnp.where(at, p, rows[PARENT])
+            rows[OCTANT] = jnp.where(at, o, rows[OCTANT])
+            k = k + jnp.where(own, 1, 0)
+        rows[LAST] = jnp.where(lanes == p, jnp.clip(k - 1, 0, n - 1), rows[LAST])
+        rows[HAS] = jnp.where(lanes == p, jnp.where(k > first, 1, 0), rows[HAS])
+        return (k, *rows)
+
+    none = jnp.zeros((1, 128), I32)
+    found = lax.fori_loop(0, parents, table, (jnp.int32(0), *[none] * 7))
+    for i in range(7):
+        tabv[i : i + 1, :] = found[1 + i]
+    tabv[7:8, :] = none
+    to_scalars = pltpu.make_async_copy(tabv, itab, sem_tab)
+    to_scalars.start()
 
     phi = split(phi_ref[...])
     many_children = 4
@@ -233,7 +270,7 @@
     def shifts(c):
         for j in range(1, nb):
             pf_copy(c, j).wait_recv()
-        per = 16 // pr
+        per = 2 * ROWS // pr
 
         def body(o, _):
             for d in range(nd):
@@ -242,14 +279,14 @@
                     y = v * v
                     co, si = horner(y, COS), v * horner(y, SIN)
                     for p in range(2):
-                        where = pl.ds(d * 32 + 2 * j * pr + p, pr, stride=2)
+                        where = pl.ds(d * PER + 2 * j * pr + p, pr, stride=2)
                         cc[c, o, where, :] = co
                         cs[c, o, where, :] = si
             return 0
 
         lax.fori_loop(0, OCT, body, 0)
 
-    tc, tf = theta_ref.shape
+    tf, tc = thetat_ref.shape
     tl = tc // nd
 
     def axis(shape, d):
@@ -262,17 +299,14 @@
         return (i >> 1) & (tf - 1)
 
     def polar_row(c, r):
-        r = r & (R - 1)
-        return (r >> 5) * tl + c * ROWS + ((r >> 2) & (ROWS - 1))
+        c, r = c + (r >> (R.bit_length() - 1)), r & (R - 1)
+        return (r >> (PER.bit_length() - 1)) * tl + c * ROWS + ((r >> 2) & (ROWS - 1))
 
     def masks():
-        shape = (2 * R, 4 * tf)
+        shape = (PAIR * R, 4 * tf)
         r, k = axis(shape, 0), axis(shape, 1)
-        p, plane, turned = r & 1, k & 1, r >= R
-        same_half = ((r >> 1) & 1) == jnp.where(k >= 2 * tf, 1, 0)
-        sign = jnp.where(turned & (p == 0), -1.0, 1.0)
-        hit = same_half & ((p != plane) == turned)
-        mask[...] = jnp.where(hit, sign, 0.0).astype(BF16)
+        hit = (((r >> 1) & 1) == jnp.where(k >= 2 * tf, 1, 0)) & ((r & 1) == (k & 1))
+        mask[...] = ones(shape, hit)
         shape = (4 * tf, R)
         k, r = axis(shape, 0), axis(shape, 1)
         hit = (((r >> 1) & 1) == jnp.where(k >= 2 * tf, 1, 0)) & ((r & 1) == (k & 1))
@@ -281,7 +315,7 @@
         w = ones(shape, fine_row(axis(shape, 1)) == axis(shape, 0))
         shape = (4 * tf, tf)
         wt = ones(shape, fine_row(axis(shape, 0)) == axis(shape, 1))
-        for v, out in zip(split(theta_ref[...]), (0, 1)):
+        for v, out in zip(split(thetat_ref[...].T), (0, 1)):
             wide[out] = d32(v, w).astype(BF16)
         for v, out in zip(split(thetat_ref[...]), (0, 1)):
             widet[out] = d32(wt, v).astype(BF16)
@@ -289,7 +323,7 @@
     d32 = functools.partial(jnp.dot, preferred_element_type=F32)
 
     def spread_map(c):
-        shape = (2 * R, tc)
+        shape = (PAIR * R, tc)
         pick = ones(shape, polar_row(c, axis(shape, 0)) == axis(shape, 1))
         for i, out in enumerate((th, tl_)):
             out[...] = d32(pick, wide[i]).astype(BF16) * mask[...]
@@ -297,31 +331,45 @@
     def spread_map_back(c):
         shape = (tc, R)
         pick = ones(shape, polar_row(c, axis(shape, 1)) == axis(shape, 0))
-        for i, out in enumerate((tth, ttl)):
-            out[...] = d32(widet[i], pick).astype(BF16) * maskt[...]
+        for i, source in enumerate((0, 0, 1)):
+            tth[:, i * R : (i + 1) * R] = d32(widet[source], pick).astype(BF16) * maskt[...]
+
+    gathered = set()
 
     def aggregate(c):
+        c = c // PAIR * PAIR
+        if c in gathered:
+            return
+        gathered.add(c)
+        for e in range(PAIR):
+            shifts(c + e)
         spread_map(c)
 
-        def body(kk, acc):
+        def body(kk, sums):
             k = 2 * kk
-            i0, i1 = itab[PERM + k], itab[PERM + k + 1]
+            i0, i1 = itab[PERM, k], itab[PERM, k + 1]
             rh = jnp.concatenate([alh[i0], alh[i1]], axis=1)
             rl = jnp.concatenate([all_[i0], all_[i1]], axis=1)
             v = dot3((th[...], tl_[...]), (rh, rl))
             for q in range(2):
-                o = itab[OCTS + k + q]
-                lanes = slice(q * 128, (q + 1) * 128)
-                y = cc[c, o] * v[:R, lanes] + cs[c, o] * v[R:, lanes]
-                acc = acc * ftab[k + q] + y
-                sb[k + q] = acc
-            return acc
-
-        lax.fori_loop(0, n // 2, body, jnp.zeros((R, 128), F32))
+                o, keep = itab[OCTS, k + q], itab[KEEP, k + q].astype(F32)
+                for e in range(PAIR):
+                    w = v[e * R : (e + 1) * R, q * 128 : (q + 1) * 128]
+                    sums[2 * e] = sums[2 * e] * keep + cc[c + e, o] * w
+                    sums[2 * e + 1] = sums[2 * e + 1] * keep + cs[c + e, o] * w
+                for e in range(2 * PAIR):
+                    sb[k + q, e] = sums[e]
+            return sums
+
+        lax.fori_loop(0, n // 2, body, [jnp.zeros((R, 128), F32)] * (2 * PAIR))
 
         def pick(p, _):
-            v = sb[itab[LAST + p]] * ftab[n + p]
-            part[c, :, :, p] = v.reshape(nd, GROUP, 8, 128)
+            last, has = itab[LAST, p], itab[HAS, p].astype(F32)
+            for e in range(PAIR):
+                v, w = (sb[last, 2 * e + i].reshape(nd * GROUP, 8, 128) for i in range(2))
+                below, above = neighbours(w)
+                v = (v + jnp.where(even_rows(w.shape), -below, above)) * has
+                part[c + e, :, :, p] = v.reshape(nd, GROUP, 8, 128)
             return 0
 
         lax.fori_loop(0, parents, pick, 0)
@@ -333,27 +381,25 @@
 
         lax.fori_loop(0, GROUP, body, 0)
 
-    def send_ends(c):
+    def send_end(c, j):
         @pl.when(z == 0)
         def _():
-            for d in range(nd - 1, 0, -1):
-                right_copy(c, d).start()
+            right_copy(c, nd - 1 - j).start()
 
         @pl.when(z == nd - 1)
         def _():
-            for d in range(nd - 1):
-                left_copy(c, d).start()
-
-    def hop(c, k):
-        d = nd - 1 - k
-
-        @pl.when(jnp.logical_and(z < d, z > 0))
+            left_copy(c, j).start()
+
+    def hop(c, t):
+        d, k = nd - 1 + z - t, t - (nd - 1 - z)
+
+        @pl.when(jnp.logical_and(z > 0, t >= z))
         def _():
             up_wait(c, d).wait_recv()
             add(c, d, d)
             right_copy(c, d).start()
 
-        @pl.when(jnp.logical_and(z > k, z < nd - 1))
+        @pl.when(jnp.logical_and(z < nd - 1, k >= 0))
         def _():
             up_wait(c, k).wait_recv()
             add(c, k, k)
@@ -374,8 +420,11 @@
             q_copy(c, j).start()
         qa[c, b] = part[c, z, g]
 
+    started = []
+
     def translate(c):
-        if c == 0:
+        if not started:
+            started.append(c)
             for j in range(1, GROUP):
                 far_copy(j).wait_recv()
             move = pltpu.make_async_copy(farr, fars, sem_fs)
@@ -389,8 +438,8 @@
         def stage(s, _):
             v = qa[c, s]
             below, above = neighbours(v)
-            ql[pl.ds(s * parents, parents)] = v
-            qs[pl.ds(s * parents, parents)] = jnp.where(even_rows(v.shape), below, above)
+            ql[pl.ds(s * parents, parents), 0] = v
+            ql[pl.ds(s * parents, parents), 1] = jnp.where(even_rows(v.shape), below, above)
             return 0
 
         lax.fori_loop(0, nb, stage, 0)
@@ -403,7 +452,7 @@
                     code = fars[jg, p, l]
                     f, kind = code & ((1 << bits) - 1), code >> bits
                     a = trans[c, kind]
-                    r, i = a * ql[f], a * qs[f]
+                    r, i = a * ql[f, 0], a * ql[f, 1]
                     u = r if u is None else u + r
                     w = i if w is None else w + i
                 re = u - pltpu.roll(u, 7, 0)
@@ -438,23 +487,29 @@
             down_left(c, z).start()
 
     def pass_down(c, k):
-        @pl.when(z >= k)
+        @pl.when(jnp.logical_and(z >= k, z < nd - 1))
         def _():
             down_right(c, z - k).wait_recv()
-
-            @pl.when(z < nd - 1)
-            def _():
-                down_right(c, z - k).start()
-
-        @pl.when(z + k < nd)
+            down_right(c, z - k).start()
+
+        @pl.when(jnp.logical_and(z + k < nd, z > 0))
         def _():
             down_left(c, z + k).wait_recv()
-
-            @pl.when(z > 0)
-            def _():
-                down_left(c, z + k).start()
+            down_left(c, z + k).start()
+
+    spread = []
 
     def disaggregate(c):
+        @pl.when(z == 0)
+        def _():
+            for d in range(1, nd):
+                down_left(c, d).wait_recv()
+
+        @pl.when(z == nd - 1)
+        def _():
+            for d in range(nd - 1):
+                down_right(c, d).wait_recv()
+
         spread_map_back(c)
 
         def stage(p, _):
@@ -465,24 +520,27 @@
             return 0
 
         lax.fori_loop(0, parents, stage, 0)
-        phit = split(phit_ref[...]) if c == C - 1 else None
+        spread.append(c)
+        first, last = len(spread) == 1, len(spread) == C
+        phi = split(phi_ref[...]) if last else None
 
         def body(ii, _):
             ys = []
             for q in range(2):
-                p, o = itab[PARENT + 2 * ii + q], itab[OCTANT + 2 * ii + q]
+                p, o = itab[PARENT, 2 * ii + q], itab[OCTANT, 2 * ii + q]
                 ys.append(cc[c, o] * xl[p] + cs[c, o] * kl[p])
-            v = dot3((tth[...], ttl[...]), split(jnp.concatenate(ys, axis=1)))
+            hi, lo = split(jnp.concatenate(ys, axis=1))
+            v = d32(tth[...], jnp.concatenate([hi, lo, hi], axis=0))
             for q in range(2):
                 w = v[:, q * 128 : (q + 1) * 128]
-                if c > 0:
+                if not first:
                     w = w + fa[2 * ii + q]
-                if c < C - 1:
+                if not last:
                     fa[2 * ii + q] = w
                 else:
                     half = w.shape[0] // 2
                     line = jnp.concatenate([w[:half], w[half:]], axis=1)
-                    fine_ref[2 * ii + q] = dot3(split(line), phit)
+                    fine_ref[2 * ii + q] = dot3(split(line), phi, turned=True)
             return 0
 
         lax.fori_loop(0, n // 2, body, 0)
@@ -491,38 +549,28 @@
     lax.fori_loop(0, n // many_children, along, 0)
     for c in range(C):
         phases_on(c)
-    shifts(0)
-    aggregate(0)
-    send_ends(0)
-    for s in range(C):
-        if s + 1 < C:
-            shifts(s + 1)
-            aggregate(s + 1)
-            send_ends(s + 1)
-        if s >= 1:
-            translate(s - 1)
-        if s >= 2:
-            for k in range(2, nd):
-                pass_down(s - 2, k)
-        hop(s, 0)
-        if s >= 1:
-            coarse(s - 1)
+    to_scalars.wait()
+
+    def steps(c):
+        yield functools.partial(aggregate, c)
+        for j in range(nd - 1):
+            yield functools.partial(send_end, c, j)
+        for t in range(1, nd - 1):
+            yield functools.partial(hop, c, t)
+        yield functools.partial(finish_up, c)
+        yield functools.partial(translate, c)
+        yield functools.partial(coarse, c)
         for k in range(1, nd - 1):
-            hop(s, k)
-        if s >= 2:
-            disaggregate(s - 2)
-        finish_up(s)
-        if s >= 1:
-            pass_down(s - 1, 1)
-    translate(C - 1)
-    coarse(C - 1)
-    if C >= 2:
-        for k in range(2, nd):
-            pass_down(C - 2, k)
-        disaggregate(C - 2)
-    for k in range(1, nd):
-        pass_down(C - 1, k)
-    disaggregate(C - 1)
+            yield functools.partial(pass_down, c, k)
+        yield functools.partial(disaggregate, c)
+
+    each = [list(steps(c)) for c in range(C)]
+    apart = len(each[0]) // 2
+    order = ORDERS.get((nd, C)) or [
+        c for _, c in sorted((c * apart + i, c) for c in range(C) for i in range(len(each[c])))
+    ]
+    for c in order:
+        each[c].pop(0)()
 
     for j in range(1, GROUP):
         far_copy(j).wait_send()
@@ -576,32 +624,15 @@
     nb, nd = lax.axis_size("box"), lax.axis_size("dir")
     noff = translation.shape[0]
     tl = tc // nd
+    ROWS = nb // FINE
+    GROUP = ROWS // 2
     C = tl // ROWS
     R = nd * GROUP * 8
+    PAIR = pair_of(R, C)
     bits = (nb * parents - 1).bit_length()
 
-    flat = (children % (n * nd)).reshape(-1)
-    own = lax.axis_index("dir") * n + jnp.arange(n, dtype=I32)
-    slots = jnp.arange(flat.shape[0], dtype=I32)
-    ids = jnp.arange(n, dtype=I32)
-    slot = jnp.sum(jnp.where(flat[None, :] == own[:, None], slots[None, :], 0), axis=1)
-    before = slot[None, :] < slot[:, None]
-    rank = jnp.sum(before.astype(I32), axis=1)
-    parent, octant = slot // OCT, slot % OCT
-    same = jnp.any(before & (parent[None, :] == parent[:, None]), axis=1).astype(I32)
-    at = rank[None, :] == ids[:, None]
-    packed = jnp.sum(jnp.where(at, (ids * OCT + octant)[None, :] * 2 + same[None, :], 0), axis=1)
-    boxes = jnp.arange(parents, dtype=I32)
-    upto = jnp.sum((parent[None, :] <= boxes[:, None]).astype(I32), axis=1)
-    has = jnp.any(parent[None, :] == boxes[:, None], axis=1)
-    itab = jnp.concatenate(
-        [packed // (2 * OCT), packed // 2 % OCT, parent, octant, jnp.maximum(upto - 1, 0)]
-    )
-    ftab = jnp.concatenate([(packed % 2).astype(F32), has.astype(F32)])
-    far = jnp.pad(far_boxes + (far_offsets << bits), ((0, 0), (0, 128 - many)))
-
     phases = (
-        shift_phase.reshape(OCT, C, ROWS * 2, 128).transpose(1, 0, 2, 3).reshape(C, OCT * 16, 128)
+        shift_phase.reshape(OCT, C, ROWS * 2, 128).transpose(1, 0, 2, 3).reshape(C, OCT * ROWS * 2, 128)
     )
 
     vmem, smem, hbm = (
@@ -611,8 +642,8 @@
     tile = (GROUP, parents, 8, 128)
     rows, fine_rows = C * GROUP * 8, tf * 2
     coarse_in, fine_in = pl.pallas_call(
-        functools.partial(kernel, (nb, nd, C, n, parents, many, bits)),
-        in_specs=[smem, smem] + [vmem] * 8 + [hbm],
+        functools.partial(kernel, (nb, nd, C, ROWS, n, parents, many, bits)),
+        in_specs=[smem] + [vmem] * 7 + [hbm],
         out_specs=[vmem, vmem],
         out_shape=[
             jax.ShapeDtypeStruct((parents, rows, 128), F32),
@@ -620,28 +651,28 @@
         ],
         scratch_shapes=[
             pltpu.VMEM((C, noff, 8, 128), F32),
+            pltpu.VMEM((8, 128), I32),
+            pltpu.SMEM((8, 128), I32),
             pltpu.VMEM((GROUP, parents, 128), I32),
             pltpu.SMEM((GROUP, parents, 128), I32),
-            pltpu.VMEM((C, nd, OCT * 16 // nb, 128), F32),
-            pltpu.VMEM((C, nb, nd, OCT * 16 // nb, 128), F32),
+            pltpu.VMEM((C, nd, OCT * 2 * ROWS // nb, 128), F32),
+            pltpu.VMEM((C, nb, nd, OCT * 2 * ROWS // nb, 128), F32),
             pltpu.VMEM((C, OCT, R, 128), F32),
             pltpu.VMEM((C, OCT, R, 128), F32),
             pltpu.VMEM((n, 2 * fine_rows, 128), BF16),
             pltpu.VMEM((n, 2 * fine_rows, 128), BF16),
-            pltpu.VMEM((2 * R, 4 * tf), BF16),
-            pltpu.VMEM((2 * R, 4 * tf), BF16),
-            pltpu.VMEM((4 * tf, R), BF16),
-            pltpu.VMEM((4 * tf, R), BF16),
+            pltpu.VMEM((PAIR * R, 4 * tf), BF16),
+            pltpu.VMEM((PAIR * R, 4 * tf), BF16),
+            pltpu.VMEM((4 * tf, 3 * R), BF16),
             pltpu.VMEM((2, tc, 4 * tf), BF16),
             pltpu.VMEM((2, 4 * tf, tc), BF16),
-            pltpu.VMEM((2 * R, 4 * tf), BF16),
+            pltpu.VMEM((PAIR * R, 4 * tf), BF16),
             pltpu.VMEM((4 * tf, R), BF16),
-            pltpu.VMEM((n, R, 128), F32),
+            pltpu.VMEM((n, 2 * PAIR, R, 128), F32),
             pltpu.VMEM((C, nd) + tile, F32),
             pltpu.VMEM((C, nd + 1) + tile, F32),
             pltpu.VMEM((C, nb) + tile[1:], F32),
-            pltpu.VMEM((nb * parents, 8, 128), F32),
-            pltpu.VMEM((nb * parents, 8, 128), F32),
+            pltpu.VMEM((nb * parents, 2, 8, 128), F32),
             pltpu.VMEM((C,) + tile, F32),
             pltpu.VMEM((C,) + tile, F32),
             pltpu.VMEM((C, nd) + tile, F32),
@@ -649,6 +680,7 @@
             pltpu.VMEM((parents, R, 128), F32),
             pltpu.VMEM((n, 4 * tf, 128), F32),
             dma((C,)),
+            dma,
             dma,
             dma((GROUP,)),
             dma((GROUP,)),
@@ -670,15 +702,13 @@
             collective_id=0, has_side_effects=True, vmem_limit_bytes=VMEM_BYTES
         ),
     )(
-        itab,
-        ftab,
-        far,
+        children.T,
+        far_boxes,
+        far_offsets,
         phases,
         rows_view(fine_out),
         phi_interp,
-        theta_interp,
         theta_interp.T,
-        phi_interp.T,
         rows_view(upper_in),
         rows_view(translation),
     )

time: 236 us -> 170 us (0.72)
  Pallas kernels: 222 us -> 164 us
  local copies, waits for them, and re-layouts: 10 us -> 5.47 us
  other arithmetic: 3.01 us -> 0 us
    pallas_call x1, Pallas kernels: 222 us -> 164 us  [shards(): pl.pallas_call(functools.partial(kernel, (nb, nd, C, ROWS, n, parents, ma...]
    unnamed x6 -> x4, local copies, waits for them, and re-layouts: 6.9 us -> 3.77 us
where the time goes in v2:
time: 170 us
  Pallas kernels  164 us (96%)
  local copies, waits for them, and re-layouts  5.47 us (3%)
    pallas_call x1, Pallas kernels, shards(): pl.pallas_call(functools.partial(kernel, (nb, nd, C, ROWS, n, parents, ma...  164 us
    unnamed x4, local copies, waits for them, and re-layouts  3.77 us

profile of v2, /device:TPU:0, one launch (start us, length us, event | category | flops | bytes accessed | tf_op | source)
XLA Modules:
  0.0 170.3 jit_solution(8754057122181628787)
XLA Ops:
  0.6 1.7 copy.18
  2.3 164.2 %shard_map.104 = (f32[16,128,128]{2,1,0:T(8,128)}, f32[32,128,128]{2,1,0:T(8,128)}) custom-call(s32[8,16]{1,0:T(8,128)} %bitcast.41, s32[16,28]{1,0:T(8,128)} %boxes_ref.1, s32[16,28]{1,0:T(8,128)} %kinds_ref.1, f32[8,64,128]{2,1,0:T(8,128)} %bitcast.36, f32[32,128,128]{2,1,0:T(8,128)} %bitcast.34, f32[128,256]{1,0:T(8,128)} %phi_ref.1, f32[64,128]{1,0:T(8,128)} %bitcast.40, ...), custom_call_target="tpu_custom_call" | custom-call | tf_op jit(solution)/shard_map/pallas_call | solution.py:644
  166.5 0.0 copy-start
  166.5 2.4 %copy.21 = f32[16,2,8192]{2,1,0:T(2,128)} copy(f32[16,2,8192]{2,1,0:T(2,128)} %bitcast.38) | data formatting | bytes 2097152
  168.9 0.0 copy-done
  169.0 1.3 copy.22
Async XLA Ops:
  166.5 2.5 %copy-start = (f32[32,128,128]{2,1,0:T(8,128)S(1)}, f32[32,128,128]{2,1,0:T(8,128)}, u32[]{:S(2)}) copy-start(f32[32,128,128]{2,1,0:T(8,128)} %get-tuple-element.5) | copy-start | bytes 6291460

commit v3 on v2

--- a/solution.py
+++ b/solution.py
@@ -12,7 +12,7 @@
 VMEM_BYTES = 60 * 1024 * 1024
 FINE = 2
 ORDERS = {
-    (4, 8): (0, 0, 0, 0, 1, 0, 3, 1, 1, 0, 3, 1, 3, 5, 1, 2, 1, 2, 3, 2, 0, 2, 3, 1, 0, 2, 3, 1, 2, 5, 3, 0, 1, 5, 2, 4, 0, 5, 5, 2, 4, 0, 4, 1, 7, 4, 2, 3, 4, 5, 0, 3, 6, 4, 5, 6, 1, 7, 6, 3, 4, 6, 7, 6, 7, 5, 3, 2, 7, 1, 6, 3, 2, 4, 6, 7, 2, 5, 7, 4, 6, 5, 6, 7, 5, 4, 6, 7, 5, 6, 4, 7, 6, 4, 7, 7),
+    (4, 8): (0, 0, 0, 0, 1, 1, 7, 0, 7, 1, 7, 2, 0, 2, 5, 3, 7, 1, 7, 2, 0, 5, 1, 5, 7, 3, 2, 2, 5, 0, 1, 7, 2, 1, 5, 4, 0, 3, 7, 6, 3, 3, 5, 1, 4, 2, 7, 4, 1, 0, 3, 2, 4, 5, 0, 6, 4, 2, 7, 3, 0, 4, 6, 1, 5, 6, 7, 3, 6, 5, 2, 4, 7, 6, 3, 2, 5, 4, 6, 4, 5, 3, 2, 4, 6, 3, 1, 5, 6, 1, 4, 3, 6, 4, 6, 6),
     (4, 4): (2, 2, 0, 0, 2, 0, 1, 2, 0, 1, 0, 2, 0, 2, 3, 0, 1, 3, 1, 1, 2, 0, 3, 1, 3, 2, 3, 0, 2, 1, 3, 1, 0, 1, 3, 2, 0, 3, 1, 2, 3, 1, 0, 2, 3, 1, 3, 3),
 }
 OCT = 8
@@ -85,13 +85,15 @@
     boxes_ref,
     kinds_ref,
     phase_ref,
-    x_ref,
+    x_hbm,
     phi_ref,
     thetat_ref,
-    upper_ref,
+    upper_hbm,
     trans_ref,
     coarse_ref,
     fine_ref,
+    x_ref,
+    upper_ref,
     trans,
     tabv,
     itab,
@@ -101,6 +103,7 @@
     pf,
     cc,
     cs,
+    flat,
     alh,
     all_,
     th,
@@ -121,6 +124,8 @@
     xl,
     kl,
     fa,
+    sem_x,
+    sem_u,
     sem_tr,
     sem_fs,
     sem_tab,
@@ -140,14 +145,14 @@
     dl_s,
     d_r,
 ):
-    nb, nd, C, ROWS, n, parents, many, bits = dims
+    nb, nd, C, ROWS, n, parents, many = dims
     GROUP = ROWS // 2
     PER = GROUP * 8
     R = nd * PER
     PAIR = pair_of(R, C)
     b, z = lax.axis_index("box"), lax.axis_index("dir")
     g, h = b % GROUP, b // GROUP
-    pr = OCT * 2 * ROWS // nb
+    own_tiles = 2 * ROWS // nb
     PERM, OCTS, PARENT, OCTANT, LAST, KEEP, HAS = range(7)
 
     def remote(src, dst, ss, rs, dev):
@@ -158,7 +163,7 @@
     def zp_copy(c, j):
         to = (z + j) % nd
         return remote(
-            phase_ref.at[c, pl.ds(pl.multiple_of(b * pr, 8), pr)],
+            phase_ref.at[pl.ds(c * 2 * ROWS + b * own_tiles, own_tiles)],
             zp.at[c, z],
             zp_s.at[c, j],
             zp_r.at[c, j],
@@ -200,10 +205,15 @@
         row = pl.multiple_of((c * GROUP + g) * 8, 8)
         return pltpu.make_async_copy(trans_ref.at[:, pl.ds(row, 8)], trans.at[c], sem_tr.at[c])
 
+    x_in = pltpu.make_async_copy(x_hbm, x_ref, sem_x)
+    upper_in = pltpu.make_async_copy(upper_hbm, upper_ref, sem_u)
+    x_in.start()
+    upper_in.start()
     for c in range(C):
         trans_copy(c).start()
 
-    farr[g, :, 0:many] = boxes_ref[...] + (kinds_ref[...] << bits)
+    farr[g, :, 0:many] = boxes_ref[...]
+    farr[g, :, 64 : 64 + many] = kinds_ref[...]
     barrier = pltpu.get_barrier_semaphore()
     for j in range(1, nb):
         pl.semaphore_signal(barrier, inc=1, device_id=(b ^ j, z), device_id_type=MESH)
@@ -217,7 +227,7 @@
     for j in range(1, GROUP):
         far_copy(j).start()
     for c in range(C):
-        zp[c, z] = phase_ref[c, pl.ds(pl.multiple_of(b * pr, 8), pr), :]
+        zp[c, z] = phase_ref[pl.ds(c * 2 * ROWS + b * own_tiles, own_tiles)]
 
     lanes = lax.broadcasted_iota(I32, (1, 128), 1)
 
@@ -270,21 +280,30 @@
     def shifts(c):
         for j in range(1, nb):
             pf_copy(c, j).wait_recv()
-        per = 2 * ROWS // pr
-
-        def body(o, _):
+        def body(i, _):
             for d in range(nd):
-                for j in range(per):
-                    v = pf[c, o * per + j, d]
+                for j in range(own_tiles):
+                    v = pf[c, i, d, j]
                     y = v * v
                     co, si = horner(y, COS), v * horner(y, SIN)
                     for p in range(2):
-                        where = pl.ds(d * PER + 2 * j * pr + p, pr, stride=2)
-                        cc[c, o, where, :] = co
-                        cs[c, o, where, :] = si
+                        row = d * PER + 2 * (i * own_tiles + j) + p
+                        flat[0, pl.ds(row, OCT, stride=R), :] = co
+                        flat[1, pl.ds(row, OCT, stride=R), :] = si
             return 0
 
-        lax.fori_loop(0, OCT, body, 0)
+        lax.fori_loop(0, nb, body, 0)
+
+        def place(o, _):
+            rows = pl.ds(pl.multiple_of(o * R, 8), R)
+            cc[c, o] = flat[0, rows, :]
+            cs[c, o] = flat[1, rows, :]
+            return 0
+
+        lax.fori_loop(0, OCT, place, 0)
+
+    def turn(c, o):
+        return cc[c, o], cs[c, o]
 
     tf, tc = thetat_ref.shape
     tl = tc // nd
@@ -355,8 +374,8 @@
                 o, keep = itab[OCTS, k + q], itab[KEEP, k + q].astype(F32)
                 for e in range(PAIR):
                     w = v[e * R : (e + 1) * R, q * 128 : (q + 1) * 128]
-                    sums[2 * e] = sums[2 * e] * keep + cc[c + e, o] * w
-                    sums[2 * e + 1] = sums[2 * e + 1] * keep + cs[c + e, o] * w
+                    for i, m in enumerate(turn(c + e, o)):
+                        sums[2 * e + i] = sums[2 * e + i] * keep + m * w
                 for e in range(2 * PAIR):
                     sb[k + q, e] = sums[e]
             return sums
@@ -449,8 +468,7 @@
             def body(p, _):
                 u = w = None
                 for l in range(many):
-                    code = fars[jg, p, l]
-                    f, kind = code & ((1 << bits) - 1), code >> bits
+                    f, kind = fars[jg, p, l], fars[jg, p, 64 + l]
                     a = trans[c, kind]
                     r, i = a * ql[f, 0], a * ql[f, 1]
                     u = r if u is None else u + r
@@ -524,32 +542,39 @@
         first, last = len(spread) == 1, len(spread) == C
         phi = split(phi_ref[...]) if last else None
 
-        def body(ii, _):
+        def pair(i):
             ys = []
             for q in range(2):
-                p, o = itab[PARENT, 2 * ii + q], itab[OCTANT, 2 * ii + q]
-                ys.append(cc[c, o] * xl[p] + cs[c, o] * kl[p])
+                p, o = itab[PARENT, i + q], itab[OCTANT, i + q]
+                co, si = turn(c, o)
+                ys.append(co * xl[p] + si * kl[p])
             hi, lo = split(jnp.concatenate(ys, axis=1))
-            v = d32(tth[...], jnp.concatenate([hi, lo, hi], axis=0))
-            for q in range(2):
-                w = v[:, q * 128 : (q + 1) * 128]
+            return d32(tth[...], jnp.concatenate([hi, lo, hi], axis=0))
+
+        def body(ii, _):
+            pairs = [pair(4 * ii), pair(4 * ii + 2)]
+            for q in range(4):
+                i = 4 * ii + q
+                w = pairs[q // 2][:, q % 2 * 128 : (q % 2 + 1) * 128]
                 if not first:
-                    w = w + fa[2 * ii + q]
+                    w = w + fa[i]
                 if not last:
-                    fa[2 * ii + q] = w
+                    fa[i] = w
                 else:
                     half = w.shape[0] // 2
                     line = jnp.concatenate([w[:half], w[half:]], axis=1)
-                    fine_ref[2 * ii + q] = dot3(split(line), phi, turned=True)
+                    fine_ref[i] = dot3(split(line), phi, turned=True)
             return 0
 
-        lax.fori_loop(0, n // 2, body, 0)
+        lax.fori_loop(0, n // 4, body, 0)
 
     masks()
-    lax.fori_loop(0, n // many_children, along, 0)
     for c in range(C):
         phases_on(c)
+    x_in.wait()
+    lax.fori_loop(0, n // many_children, along, 0)
     to_scalars.wait()
+    upper_in.wait()
 
     def steps(c):
         yield functools.partial(aggregate, c)
@@ -629,11 +654,8 @@
     C = tl // ROWS
     R = nd * GROUP * 8
     PAIR = pair_of(R, C)
-    bits = (nb * parents - 1).bit_length()
-
-    phases = (
-        shift_phase.reshape(OCT, C, ROWS * 2, 128).transpose(1, 0, 2, 3).reshape(C, OCT * ROWS * 2, 128)
-    )
+
+    phases = shift_phase.reshape(OCT, tl * 2, 128).transpose(1, 0, 2)
 
     vmem, smem, hbm = (
         pl.BlockSpec(memory_space=m) for m in (pltpu.VMEM, pltpu.SMEM, pl.ANY)
@@ -642,23 +664,26 @@
     tile = (GROUP, parents, 8, 128)
     rows, fine_rows = C * GROUP * 8, tf * 2
     coarse_in, fine_in = pl.pallas_call(
-        functools.partial(kernel, (nb, nd, C, ROWS, n, parents, many, bits)),
-        in_specs=[smem] + [vmem] * 7 + [hbm],
+        functools.partial(kernel, (nb, nd, C, ROWS, n, parents, many)),
+        in_specs=[smem] + [vmem] * 3 + [hbm] + [vmem] * 2 + [hbm] * 2,
         out_specs=[vmem, vmem],
         out_shape=[
             jax.ShapeDtypeStruct((parents, rows, 128), F32),
             jax.ShapeDtypeStruct((n, fine_rows, pf_), F32),
         ],
         scratch_shapes=[
+            pltpu.VMEM((n, fine_rows, pf_), F32),
+            pltpu.VMEM((parents, rows, 128), F32),
             pltpu.VMEM((C, noff, 8, 128), F32),
             pltpu.VMEM((8, 128), I32),
             pltpu.SMEM((8, 128), I32),
             pltpu.VMEM((GROUP, parents, 128), I32),
             pltpu.SMEM((GROUP, parents, 128), I32),
-            pltpu.VMEM((C, nd, OCT * 2 * ROWS // nb, 128), F32),
-            pltpu.VMEM((C, nb, nd, OCT * 2 * ROWS // nb, 128), F32),
+            pltpu.VMEM((C, nd, 2 * ROWS // nb, OCT, 128), F32),
+            pltpu.VMEM((C, nb, nd, 2 * ROWS // nb, OCT, 128), F32),
             pltpu.VMEM((C, OCT, R, 128), F32),
             pltpu.VMEM((C, OCT, R, 128), F32),
+            pltpu.VMEM((2, OCT * R, 128), F32),
             pltpu.VMEM((n, 2 * fine_rows, 128), BF16),
             pltpu.VMEM((n, 2 * fine_rows, 128), BF16),
             pltpu.VMEM((PAIR * R, 4 * tf), BF16),
@@ -679,6 +704,8 @@
             pltpu.VMEM((parents, R, 128), F32),
             pltpu.VMEM((parents, R, 128), F32),
             pltpu.VMEM((n, 4 * tf, 128), F32),
+            dma,
+            dma,
             dma((C,)),
             dma,
             dma,

time: 170 us -> 157 us (0.924)
  Pallas kernels: 164 us -> 153 us
    pallas_call x1, Pallas kernels: 164 us -> 153 us  [shards(): pl.pallas_call(functools.partial(kernel, (nb, nd, C, ROWS, n, parents, ma...]
    reshape x1 -> x0, local copies, waits for them, and re-layouts: 1.7 us -> none  [shards(): shift_phase.reshape(OCT, C, ROWS * 2, 128).transpose(1, 0, 2, 3)]
where the time goes in v3:
time: 157 us
  Pallas kernels  153 us (97%)
  local copies, waits for them, and re-layouts  3.77 us (2%)
    pallas_call x1, Pallas kernels, shards(): pl.pallas_call(functools.partial(kernel, (nb, nd, C, ROWS, n, parents, ma...  153 us
    unnamed x4, local copies, waits for them, and re-layouts  3.77 us

profile of v3, /device:TPU:0, one launch (start us, length us, event | category | flops | bytes accessed | tf_op | source)
XLA Modules:
  0.0 157.3 jit_solution(10963709479240180343)
XLA Ops:
  0.6 152.9 %shard_map.104 = (f32[16,128,128]{2,1,0:T(8,128)}, f32[32,128,128]{2,1,0:T(8,128)}) custom-call(s32[8,16]{1,0:T(8,128)} %bitcast.37, s32[16,28]{1,0:T(8,128)} %boxes_ref.1, s32[16,28]{1,0:T(8,128)} %kinds_ref.1, f32[64,8,128]{2,1,0:T(8,128)} %bitcast.35, f32[32,128,128]{2,1,0:T(8,128)} %bitcast.31, f32[128,256]{1,0:T(8,128)} %phi_ref.1, f32[64,128]{1,0:T(8,128)} %bitcast.36, ...), custom_call_target="tpu_custom_call" | custom-call | tf_op jit(solution)/shard_map/pallas_call | solution.py:666
  153.5 0.0 copy-start
  153.5 2.4 %copy.18 = f32[16,2,8192]{2,1,0:T(2,128)} copy(f32[16,2,8192]{2,1,0:T(2,128)} %bitcast.34) | data formatting | bytes 2097152
  156.0 0.0 copy-done
  156.0 1.3 copy.19
Async XLA Ops:
  153.5 2.5 %copy-start = (f32[32,128,128]{2,1,0:T(8,128)S(1)}, f32[32,128,128]{2,1,0:T(8,128)}, u32[]{:S(2)}) copy-start(f32[32,128,128]{2,1,0:T(8,128)} %get-tuple-element.5) | copy-start | bytes 6291460

commit v4 on v3

--- a/solution.py
+++ b/solution.py
@@ -90,6 +90,8 @@
     thetat_ref,
     upper_hbm,
     trans_ref,
+    coarse_hbm,
+    fine_hbm,
     coarse_ref,
     fine_ref,
     x_ref,
@@ -126,6 +128,8 @@
     fa,
     sem_x,
     sem_u,
+    sem_c,
+    sem_f,
     sem_tr,
     sem_fs,
     sem_tab,
@@ -153,6 +157,10 @@
     b, z = lax.axis_index("box"), lax.axis_index("dir")
     g, h = b % GROUP, b // GROUP
     own_tiles = 2 * ROWS // nb
+    count = 3 * nd
+    order = ORDERS.get((nd, C)) or [
+        c for _, c in sorted((c * (count // 2) + i, c) for c in range(C) for i in range(count))
+    ]
     PERM, OCTS, PARENT, OCTANT, LAST, KEEP, HAS = range(7)
 
     def remote(src, dst, ss, rs, dev):
@@ -221,7 +229,8 @@
         pl.semaphore_signal(barrier, inc=1, device_id=(b, (z + j) % nd), device_id_type=MESH)
     pl.semaphore_wait(barrier, nb + nd - 2)
 
-    for c in range(C):
+    use = [q for p in dict.fromkeys(c // PAIR for c in order) for q in range(p * PAIR, (p + 1) * PAIR)]
+    for c in use:
         for j in range(1, nd):
             zp_copy(c, j).start()
     for j in range(1, GROUP):
@@ -483,6 +492,10 @@
             t_copy(c, j).start()
         ta[c, g] = ts[c, g]
 
+    def coarse_out(c):
+        rows = pl.ds(c * PER, PER)
+        return pltpu.make_async_copy(coarse_ref.at[:, rows], coarse_hbm.at[:, rows], sem_c.at[c])
+
     def coarse(c):
         for j in range(1, GROUP):
             t_copy(c, j).wait_recv()
@@ -495,6 +508,7 @@
             return 0
 
         lax.fori_loop(0, parents, body, 0)
+        coarse_out(c).start()
 
         @pl.when(z < nd - 1)
         def _():
@@ -564,12 +578,15 @@
                     half = w.shape[0] // 2
                     line = jnp.concatenate([w[:half], w[half:]], axis=1)
                     fine_ref[i] = dot3(split(line), phi, turned=True)
+            if last:
+                done = pl.ds(4 * ii, 4)
+                pltpu.make_async_copy(fine_ref.at[done], fine_hbm.at[done], sem_f).start()
             return 0
 
         lax.fori_loop(0, n // 4, body, 0)
 
     masks()
-    for c in range(C):
+    for c in use:
         phases_on(c)
     x_in.wait()
     lax.fori_loop(0, n // many_children, along, 0)
@@ -590,12 +607,13 @@
         yield functools.partial(disaggregate, c)
 
     each = [list(steps(c)) for c in range(C)]
-    apart = len(each[0]) // 2
-    order = ORDERS.get((nd, C)) or [
-        c for _, c in sorted((c * apart + i, c) for c in range(C) for i in range(len(each[c])))
-    ]
     for c in order:
         each[c].pop(0)()
+    assert not any(each)
+
+    pltpu.make_async_copy(fine_ref, fine_hbm, sem_f).wait()
+    for c in range(C):
+        coarse_out(c).wait()
 
     for j in range(1, GROUP):
         far_copy(j).wait_send()
@@ -666,12 +684,14 @@
     coarse_in, fine_in = pl.pallas_call(
         functools.partial(kernel, (nb, nd, C, ROWS, n, parents, many)),
         in_specs=[smem] + [vmem] * 3 + [hbm] + [vmem] * 2 + [hbm] * 2,
-        out_specs=[vmem, vmem],
+        out_specs=[hbm, hbm],
         out_shape=[
             jax.ShapeDtypeStruct((parents, rows, 128), F32),
             jax.ShapeDtypeStruct((n, fine_rows, pf_), F32),
         ],
         scratch_shapes=[
+            pltpu.VMEM((parents, rows, 128), F32),
+            pltpu.VMEM((n, fine_rows, pf_), F32),
             pltpu.VMEM((n, fine_rows, pf_), F32),
             pltpu.VMEM((parents, rows, 128), F32),
             pltpu.VMEM((C, noff, 8, 128), F32),
@@ -708,6 +728,8 @@
             dma,
             dma((C,)),
             dma,
+            dma((C,)),
+            dma,
             dma,
             dma((GROUP,)),
             dma((GROUP,)),

time: 157 us -> 157 us (level)
  no operation moved by 1% of the time
where the time goes in v4:
time: 157 us; the launch traced here: 156 us
  Pallas kernels  152 us (97%)
  local copies, waits for them, and re-layouts  3.77 us (2%)
    pallas_call x1, Pallas kernels, shards(): pl.pallas_call(functools.partial(kernel, (nb, nd, C, ROWS, n, parents, ma...  152 us
    unnamed x4, local copies, waits for them, and re-layouts  3.77 us

profile of v4, /device:TPU:0, one launch (start us, length us, event | category | flops | bytes accessed | tf_op | source)
XLA Modules:
  0.0 156.4 jit_solution(5448148086141870083)
XLA Ops:
  0.6 152.0 %shard_map.104 = (f32[16,128,128]{2,1,0:T(8,128)}, f32[32,128,128]{2,1,0:T(8,128)}) custom-call(s32[8,16]{1,0:T(8,128)} %bitcast.37, s32[16,28]{1,0:T(8,128)} %boxes_ref.1, s32[16,28]{1,0:T(8,128)} %kinds_ref.1, f32[64,8,128]{2,1,0:T(8,128)} %bitcast.35, f32[32,128,128]{2,1,0:T(8,128)} %bitcast.31, f32[128,256]{1,0:T(8,128)} %phi_ref.1, f32[64,128]{1,0:T(8,128)} %bitcast.36, ...), custom_call_target="tpu_custom_call" | custom-call | tf_op jit(solution)/shard_map/pallas_call | solution.py:684
  152.7 0.0 copy-start
  152.7 2.4 %copy.18 = f32[16,2,8192]{2,1,0:T(2,128)} copy(f32[16,2,8192]{2,1,0:T(2,128)} %bitcast.34) | data formatting | bytes 2097152
  155.1 0.0 copy-done
  155.1 1.3 copy.19
Async XLA Ops:
  152.7 2.5 %copy-start = (f32[32,128,128]{2,1,0:T(8,128)S(1)}, f32[32,128,128]{2,1,0:T(8,128)}, u32[]{:S(2)}) copy-start(f32[32,128,128]{2,1,0:T(8,128)} %get-tuple-element.5) | copy-start | bytes 6291460

commit v5 on v4

--- a/solution.py
+++ b/solution.py
@@ -12,7 +12,7 @@
 VMEM_BYTES = 60 * 1024 * 1024
 FINE = 2
 ORDERS = {
-    (4, 8): (0, 0, 0, 0, 1, 1, 7, 0, 7, 1, 7, 2, 0, 2, 5, 3, 7, 1, 7, 2, 0, 5, 1, 5, 7, 3, 2, 2, 5, 0, 1, 7, 2, 1, 5, 4, 0, 3, 7, 6, 3, 3, 5, 1, 4, 2, 7, 4, 1, 0, 3, 2, 4, 5, 0, 6, 4, 2, 7, 3, 0, 4, 6, 1, 5, 6, 7, 3, 6, 5, 2, 4, 7, 6, 3, 2, 5, 4, 6, 4, 5, 3, 2, 4, 6, 3, 1, 5, 6, 1, 4, 3, 6, 4, 6, 6),
+    (4, 8): (0, 1, 1, 0, 1, 1, 0, 2, 1, 0, 2, 0, 3, 3, 1, 5, 0, 2, 1, 3, 2, 3, 2, 4, 0, 3, 1, 5, 2, 3, 0, 2, 1, 3, 0, 5, 4, 5, 5, 4, 4, 6, 1, 0, 7, 2, 5, 4, 2, 0, 6, 7, 6, 7, 3, 5, 4, 6, 3, 0, 2, 4, 6, 7, 1, 5, 7, 2, 6, 4, 7, 5, 6, 4, 3, 7, 2, 5, 6, 3, 4, 7, 6, 3, 7, 4, 6, 1, 4, 6, 5, 7, 6, 5, 7, 7),
     (4, 4): (2, 2, 0, 0, 2, 0, 1, 2, 0, 1, 0, 2, 0, 2, 3, 0, 1, 3, 1, 1, 2, 0, 3, 1, 3, 2, 3, 0, 2, 1, 3, 1, 0, 1, 3, 2, 0, 3, 1, 2, 3, 1, 0, 2, 3, 1, 3, 3),
 }
 OCT = 8

time: 157 us -> 155 us (0.987)
  Pallas kernels: 152 us -> 150 us
    pallas_call x1, Pallas kernels: 152 us -> 150 us  [shards(): pl.pallas_call(functools.partial(kernel, (nb, nd, C, ROWS, n, parents, ma...]
where the time goes in v5:
time: 155 us
  Pallas kernels  150 us (97%)
  local copies, waits for them, and re-layouts  3.77 us (2%)
    pallas_call x1, Pallas kernels, shards(): pl.pallas_call(functools.partial(kernel, (nb, nd, C, ROWS, n, parents, ma...  150 us
    unnamed x4, local copies, waits for them, and re-layouts  3.77 us

profile of v5, /device:TPU:0, one launch (start us, length us, event | category | flops | bytes accessed | tf_op | source)
XLA Modules:
  0.0 154.7 jit_solution(16393359601509698324)
XLA Ops:
  0.6 150.3 %shard_map.104 = (f32[16,128,128]{2,1,0:T(8,128)}, f32[32,128,128]{2,1,0:T(8,128)}) custom-call(s32[8,16]{1,0:T(8,128)} %bitcast.37, s32[16,28]{1,0:T(8,128)} %boxes_ref.1, s32[16,28]{1,0:T(8,128)} %kinds_ref.1, f32[64,8,128]{2,1,0:T(8,128)} %bitcast.35, f32[32,128,128]{2,1,0:T(8,128)} %bitcast.31, f32[128,256]{1,0:T(8,128)} %phi_ref.1, f32[64,128]{1,0:T(8,128)} %bitcast.36, ...), custom_call_target="tpu_custom_call" | custom-call | tf_op jit(solution)/shard_map/pallas_call | solution.py:684
  150.9 0.0 copy-start
  150.9 2.4 %copy.18 = f32[16,2,8192]{2,1,0:T(2,128)} copy(f32[16,2,8192]{2,1,0:T(2,128)} %bitcast.34) | data formatting | bytes 2097152
  153.4 0.0 copy-done
  153.4 1.3 copy.19
Async XLA Ops:
  150.9 2.5 %copy-start = (f32[32,128,128]{2,1,0:T(8,128)S(1)}, f32[32,128,128]{2,1,0:T(8,128)}, u32[]{:S(2)}) copy-start(f32[32,128,128]{2,1,0:T(8,128)} %get-tuple-element.5) | copy-start | bytes 6291460

commit v6 on v5

--- a/solution.py
+++ b/solution.py
@@ -289,6 +289,7 @@
     def shifts(c):
         for j in range(1, nb):
             pf_copy(c, j).wait_recv()
+
         def body(i, _):
             for d in range(nd):
                 for j in range(own_tiles):
@@ -586,10 +587,12 @@
         lax.fori_loop(0, n // 4, body, 0)
 
     masks()
-    for c in use:
+    for c in use[:PAIR]:
         phases_on(c)
     x_in.wait()
     lax.fori_loop(0, n // many_children, along, 0)
+    for c in use[PAIR:]:
+        phases_on(c)
     to_scalars.wait()
     upper_in.wait()
 

time: 155 us -> 153 us (0.987)
  Pallas kernels: 150 us -> 148 us
    pallas_call x1, Pallas kernels: 150 us -> 148 us  [shards(): pl.pallas_call(functools.partial(kernel, (nb, nd, C, ROWS, n, parents, ma...]
where the time goes in v6:
time: 153 us
  Pallas kernels  148 us (97%)
  local copies, waits for them, and re-layouts  3.77 us (2%)
    pallas_call x1, Pallas kernels, shards(): pl.pallas_call(functools.partial(kernel, (nb, nd, C, ROWS, n, parents, ma...  148 us
    unnamed x4, local copies, waits for them, and re-layouts  3.77 us

profile of v6, /device:TPU:0, one launch (start us, length us, event | category | flops | bytes accessed | tf_op | source)
XLA Modules:
  0.0 152.9 jit_solution(4164800459800216269)
XLA Ops:
  0.6 148.5 %shard_map.104 = (f32[16,128,128]{2,1,0:T(8,128)}, f32[32,128,128]{2,1,0:T(8,128)}) custom-call(s32[8,16]{1,0:T(8,128)} %bitcast.37, s32[16,28]{1,0:T(8,128)} %boxes_ref.1, s32[16,28]{1,0:T(8,128)} %kinds_ref.1, f32[64,8,128]{2,1,0:T(8,128)} %bitcast.35, f32[32,128,128]{2,1,0:T(8,128)} %bitcast.31, f32[128,256]{1,0:T(8,128)} %phi_ref.1, f32[64,128]{1,0:T(8,128)} %bitcast.36, ...), custom_call_target="tpu_custom_call" | custom-call | tf_op jit(solution)/shard_map/pallas_call | solution.py:687
  149.1 0.0 copy-start
  149.1 2.4 %copy.18 = f32[16,2,8192]{2,1,0:T(2,128)} copy(f32[16,2,8192]{2,1,0:T(2,128)} %bitcast.34) | data formatting | bytes 2097152
  151.6 0.0 copy-done
  151.6 1.3 copy.19
Async XLA Ops:
  149.1 2.5 %copy-start = (f32[32,128,128]{2,1,0:T(8,128)S(1)}, f32[32,128,128]{2,1,0:T(8,128)}, u32[]{:S(2)}) copy-start(f32[32,128,128]{2,1,0:T(8,128)} %get-tuple-element.5) | copy-start | bytes 6291460
